TPU v7x, 256 devices: a whole 4x4x8 slice. The times are simulated.
256 devices in a mesh: batch: 16 (over z, core), feat: 16 (over y, x).
Axes of the slice: x: 4, y: 4, z: 8, core: 2. Of those that a mesh axis runs over, the one named last changes fastest.
Arguments:
- noise: bfloat16 [128, 1048576], P('batch', 'feat'), may hold values from -7 to 7
- data: bfloat16 [128, 1048576], P('batch', 'feat'), may hold values from -5 to 5
Outputs:
- targets: bfloat16 [128, 1048576], P('batch', 'feat')
- row_potential: float32 [128], P('batch')
- column_potential: float32 [128], replicated
All inputs are finite; a program needn't handle non-finite values.
Results may differ from a plain program's by a relative error of at most 0.012.
Values may be sent and summed in bfloat16 or wider, within the bound.
A program may use at most 64 MiB of HBM per device.

v0:
```python
import math

import jax
import jax.numpy as jnp
from jax import lax
from jax.sharding import PartitionSpec as P

F = 1048576
ITERS = 3


def row_lse(values, axis):
    top = jnp.max(values, axis=axis, keepdims=True)
    return jnp.squeeze(top, axis) + jnp.log(jnp.sum(jnp.exp(values - top), axis=axis))


def inner_rows(left, right):
    return lax.dot_general(
        left, right, (((1,), (1,)), ((), ())), preferred_element_type=jnp.float32
    )


def per_device(noise, data):
    rows, width = noise.shape
    total_rows = rows * lax.axis_size("batch")
    root = math.sqrt(F)
    log_count = math.log(total_rows)
    noise_norm = jnp.sum(jnp.square(noise.astype(jnp.float32)), axis=1)
    gathered = lax.all_gather(data, "batch", axis=0, tiled=True)
    cross = inner_rows(noise, gathered)
    data_norm = jnp.sum(jnp.square(gathered.astype(jnp.float32)), axis=1)
    cross, noise_norm, data_norm = lax.psum((cross, noise_norm, data_norm), "feat")
    scores = (2.0 * cross - noise_norm[:, None] - data_norm[None, :]) / root + 2.0 * root
    row_potential = jnp.zeros((rows,), jnp.float32)
    column_potential = jnp.zeros((total_rows,), jnp.float32)
    for step in range(ITERS):
        row_potential = -log_count - row_lse(scores + column_potential[None, :], 1)
        shifted = scores + row_potential[:, None]
        local_top = jnp.max(shifted, axis=0)
        top = lax.pmax(local_top, "batch")
        total = lax.psum(jnp.sum(jnp.exp(shifted - top[None, :]), axis=0), "batch")
        column_potential = -log_count - (top + jnp.log(total))
    plan = jnp.exp(scores + row_potential[:, None] + column_potential[None, :])
    weights = (plan / jnp.sum(plan, axis=1, keepdims=True)).astype(jnp.bfloat16)
    summed = jnp.dot(weights, gathered, preferred_element_type=jnp.float32)
    return (summed.astype(jnp.bfloat16), row_potential, column_potential)


def solution(mesh):
    placed = (P("batch", "feat"), P("batch", "feat"))
    return jax.shard_map(
        per_device,
        mesh=mesh,
        in_specs=placed,
        out_specs=(P("batch", "feat"), P("batch"), P()),
        check_vma=False,
    )
```

profile of v0, /device:TPU:1, one launch (start us, length us, event | category | flops | bytes accessed | tf_op | source)
XLA Modules:
  0.0 324.1 jit_solution(11855591943470860464)
XLA Ops:
  7.2 0.0 copy-start
  7.2 0.0 all-gather.2.cloned.1.call-start
  7.2 0.7 all-gather.2.cloned.1.call-update
  7.9 1.9 multiply_reduce_fusion.1
  9.8 99.7 %all-gather.2.cloned.1.call-done = bf16[128,65536]{1,0:T(8,128)(2,1)} async-done(((bf16[8,65536]{1,0:T(8,128)(2,1)}), bf16[128,65536]{1,0:T(8,128)(2,1)}) %all-gather.2.cloned.1.call-update) | async-done | bytes 16777232 | tf_op jit(solution)/shard_map/all_gather | solution.py:29
  109.5 7.2 %multiply_reduce_fusion = f32[128]{0:T(128)S(1)} fusion(bf16[128,65536]{1,0:T(8,128)(2,1)} %all-gather.2.cloned.1.call-done), kind=kLoop, calls=%fused_computation.1 | loop fusion | flops 25165696 | bytes 16777728 | tf_op jit(solution)/shard_map/reduce_sum | solution.py:31
  116.7 0.0 copy-done
  116.7 8.0 %fusion.5 = f32[8,128]{1,0:T(8,128)S(1)} fusion(bf16[8,65536]{1,0:T(8,128)(2,1)S(1)} %copy-done, bf16[128,65536]{1,0:T(8,128)(2,1)} %all-gather.2.cloned.1.call-done), kind=kOutput, calls=%fused_computation.28 | convolution fusion | flops 134217728 | bytes 17829888 | tf_op jit(solution)/shard_map/dot_general | solution.py:18
  124.7 33.7 %all-reduce = (f32[8,128]{1,0:T(8,128)S(1)}, f32[128]{0:T(128)S(1)}, f32[8]{0:T(128)S(1)}) all-reduce(f32[8,128]{1,0:T(8,128)S(1)} %fusion.5, f32[128]{0:T(128)S(1)} %multiply_reduce_fusion, f32[8]{0:T(128)S(1)} %multiply_reduce_fusion.1), channel_id=1, replica_groups=mesh['batch'=16,'feat'=16] {'feat'}, use_global_device_ids=true, to_apply=%region_0.0 | all-reduce | flops 1160 | bytes 9280 | tf_op jit(solution)/shard_map/psum | solution.py:32
  158.4 0.2 fusion.4
  158.6 0.2 exponential_reduce_fusion.5
  158.8 0.1 add_reduce_fusion.3
  158.9 30.3 %pmax.21 = f32[128]{0:T(128)S(1)} all-reduce(f32[128]{0:T(128)S(1)} %add_reduce_fusion.3), channel_id=1, replica_groups=mesh['batch'=16,'feat'=16] {'batch'}, use_global_device_ids=true, to_apply=%region_8.0 | all-reduce | flops 128 | bytes 1024 | tf_op jit(solution)/shard_map/pmax | solution.py:40
  189.2 0.1 exponential_reduce_fusion.4
  189.3 23.5 %psum.45 = f32[128]{0:T(128)S(1)} all-reduce(f32[128]{0:T(128)S(1)} %exponential_reduce_fusion.4), channel_id=1, replica_groups=mesh['batch'=16,'feat'=16] {'batch'}, use_global_device_ids=true, to_apply=%region_10.0 | all-reduce | flops 128 | bytes 1024 | tf_op jit(solution)/shard_map/psum | solution.py:41
  212.9 0.1 add_reduce_fusion.2
  213.0 0.2 exponential_reduce_fusion.3
  213.2 0.1 add_reduce_fusion.1
  213.3 23.5 %pmax.22 = f32[128]{0:T(128)S(1)} all-reduce(f32[128]{0:T(128)S(1)} %add_reduce_fusion.1), channel_id=1, replica_groups=mesh['batch'=16,'feat'=16] {'batch'}, use_global_device_ids=true, to_apply=%region_14.0 | all-reduce | flops 128 | bytes 1024 | tf_op jit(solution)/shard_map/pmax | solution.py:40
  236.8 0.1 exponential_reduce_fusion.2
  236.9 23.5 %psum.46 = f32[128]{0:T(128)S(1)} all-reduce(f32[128]{0:T(128)S(1)} %exponential_reduce_fusion.2), channel_id=1, replica_groups=mesh['batch'=16,'feat'=16] {'batch'}, use_global_device_ids=true, to_apply=%region_16.0 | all-reduce | flops 128 | bytes 1024 | tf_op jit(solution)/shard_map/psum | solution.py:41
  260.4 0.1 add_reduce_fusion
  260.6 0.2 exponential_reduce_fusion.1
  260.8 0.0 copy-start.1
  260.8 0.1 add_reduce_fusion.4
  260.9 23.5 %pmax.23 = f32[128]{0:T(128)S(1)} all-reduce(f32[128]{0:T(128)S(1)} %add_reduce_fusion.4), channel_id=1, replica_groups=mesh['batch'=16,'feat'=16] {'batch'}, use_global_device_ids=true, to_apply=%region_20.0 | all-reduce | flops 128 | bytes 1024 | tf_op jit(solution)/shard_map/pmax | solution.py:40
  284.4 0.1 exponential_reduce_fusion
  284.5 23.5 %psum.47 = f32[128]{0:T(128)S(1)} all-reduce(f32[128]{0:T(128)S(1)} %exponential_reduce_fusion), channel_id=1, replica_groups=mesh['batch'=16,'feat'=16] {'batch'}, use_global_device_ids=true, to_apply=%region_22.0 | all-reduce | flops 128 | bytes 1024 | tf_op jit(solution)/shard_map/psum | solution.py:41
  308.0 0.0 copy-start.2
  308.0 0.2 fusion
  308.2 9.1 %convolution_convert_fusion = bf16[8,65536]{1,0:T(8,128)(2,1)} fusion(bf16[128,65536]{1,0:T(8,128)(2,1)} %all-gather.2.cloned.1.call-done, f32[8,128]{1,0:T(8,128)S(1)} %get-tuple-element.7, f32[8]{0:T(128)S(1)} %fusion, f32[128]{0:T(128)S(1)} %add_subtract_fusion, f32[8]{0:T(128)S(1)} %add_subtract_fusion.1), kind=kOutput, calls=%fused_computation | convolution fusion | flops 134746112 | bytes 17830464 | tf_op jit(solution)/shard_map/dot_general | solution.py:45
  317.3 0.0 copy-done.1
  317.3 0.0 copy-done.2
  (6 shorter events, 0.1 us)
Async XLA Ops:
  7.2 109.5 %copy-start = (bf16[8,65536]{1,0:T(8,128)(2,1)S(1)}, bf16[8,65536]{1,0:T(8,128)(2,1)}, u32[]{:S(2)}) copy-start(bf16[8,65536]{1,0:T(8,128)(2,1)} %param.2) | copy-start | bytes 3145732
  7.2 102.3 %all-gather.2.cloned.1.call-start = ((), (), s32[]{:S(2)}) async-start(), calls=%async_computation | async-start | bytes 17825792 | tf_op jit(solution)/shard_map/all_gather | solution.py:29
  260.8 56.5 %copy-start.1 = (f32[8]{0:T(128)}, f32[8]{0:T(128)S(1)}, u32[]{:S(2)}) copy-start(f32[8]{0:T(128)S(1)} %add_subtract_fusion.1) | copy-start | bytes 100
  308.0 9.3 %copy-start.2 = (f32[128]{0:T(128)}, f32[128]{0:T(128)S(1)}, u32[]{:S(2)}) copy-start(f32[128]{0:T(128)S(1)} %add_subtract_fusion) | copy-start | bytes 1540
Sparse Core Ops, SparseCore 0:
  9.8 99.6 all-gather.1
where the time goes:
time: 324 us
  blocking collectives  182 us (56%)
  waiting for transfers between devices  100 us (31%)
  matrix products  17.1 us (5%)
  between operations  14.1 us (4%)
  other arithmetic  10.8 us (3%)
    all_gather x1, waiting for transfers between devices, per_device(): gathered = lax.all_gather(data, 'batch', axis=0, tiled=True)  99.7 us
    pmax x3, blocking collectives, per_device(): top = lax.pmax(local_top, 'batch')  77.4 us
    psum x3, blocking collectives, per_device(): total = lax.psum(jnp.sum(jnp.exp(shifted - top[None, :]), axis=0), 'batch')  70.6 us
    psum x1, blocking collectives, per_device(): lax.psum((cross, noise_norm, data_norm), 'feat')  33.7 us
    dot_general x1, matrix products, per_device(): summed = jnp.dot(weights, gathered, preferred_element_type=jnp.float32)  9.09 us
    dot_general x1, matrix products, inner_rows(): lax.dot_general(left, right, (((1,), (1,)), ((), ())), preferred_element_...  8.03 us
    reduce_sum x1, other arithmetic, per_device(): data_norm = jnp.sum(jnp.square(gathered.astype(jnp.float32)), axis=1)  7.19 us
  transfers between devices with their start and end apart: 1, of which 1 were waited for; matrix products, arithmetic and copies ran while one was open for 1% of the time, Pallas kernels for 0%

commit v1 on v0

v1 whole, which is shorter than its diff:
```python
import functools
import math

import jax
import jax.numpy as jnp
from jax import lax
from jax.experimental import pallas as pl
from jax.experimental.pallas import tpu as pltpu
from jax.sharding import PartitionSpec as P

ITERS = 3
MESH = pl.DeviceIdType.MESH


def lse(values, axis):
    top = jnp.max(values, axis=axis, keepdims=True)
    return top + jnp.log(jnp.sum(jnp.exp(values - top), axis=axis, keepdims=True))


def ring_order(count):
    offsets = sorted(range(1, count), key=lambda k: (-min(k, count - k), k))
    return offsets


def kernel(
    nb, nf, noise, data, out, row_out, col_out,
    noise_buf, data_buf, local_buf, full, obuf, part, own, a_buf, b_buf, c_buf,
    norm_own, norm_b, norm_c, pot,
    local_sem, send_sem, recv_sem, small_send, small_recv, out_send, out_recv,
):
    rows, width = noise.shape
    w = width // nb
    total = rows * nb
    features = width * nf
    root = math.sqrt(features)
    log_count = math.log(total)
    b, f = lax.axis_index("batch"), lax.axis_index("feat")
    b_order, f_order = ring_order(nb), list(range(1, nf))

    def in_column(k):
        return dict(device_id=(lax.rem(b + k, nb), f), device_id_type=MESH)

    def in_plane(k):
        return dict(device_id=(b, lax.rem(f + k, nf)), device_id_type=MESH)

    def drain(ref, sem, count):
        view = ref.at[pl.ds(0, count)]
        pltpu.make_async_copy(view, view, sem).wait()

    barrier = pltpu.get_barrier_semaphore()
    for k in b_order:
        pl.semaphore_signal(barrier, inc=1, **in_column(k))
    for k in f_order:
        pl.semaphore_signal(barrier, inc=1, **in_plane(k))
    pl.semaphore_wait(barrier, nb + nf - 2)

    for k in b_order:
        t = lax.rem(b + k, nb)
        columns = pl.ds(pl.multiple_of(t * w, w), w)
        for i, (ref, buf) in enumerate(((noise, noise_buf), (data, data_buf))):
            pltpu.make_async_remote_copy(
                src_ref=ref.at[:, columns], dst_ref=buf.at[b],
                send_sem=send_sem.at[i], recv_sem=recv_sem.at[i], **in_column(k)
            ).start()
    mine = pl.ds(pl.multiple_of(b * w, w), w)
    locals_ = [
        pltpu.make_async_copy(noise, local_buf.at[0], local_sem.at[0]),
        pltpu.make_async_copy(data, local_buf.at[1], local_sem.at[1]),
        pltpu.make_async_copy(noise.at[:, mine], noise_buf.at[b], local_sem.at[2]),
        pltpu.make_async_copy(data.at[:, mine], data_buf.at[b], local_sem.at[3]),
    ]
    for c in locals_:
        c.start()
    for c in locals_:
        c.wait()

    def exchange(src_of, buf, slot, partner, order, sem):
        for k in order:
            pltpu.make_async_remote_copy(
                src_ref=src_of(k), dst_ref=buf.at[slot],
                send_sem=small_send.at[sem], recv_sem=small_recv.at[sem], **partner(k)
            ).start()

    chunk = min(2048, width)
    for i in range(2):
        def add(step, acc, i=i):
            v = local_buf[i, :, pl.ds(pl.multiple_of(step * chunk, chunk), chunk)].astype(jnp.float32)
            v = v * v
            for q in range(chunk // 128):
                acc = acc + v[:, q * 128:(q + 1) * 128]
            return acc
        acc = lax.fori_loop(0, width // chunk, add, jnp.zeros((rows, 128), jnp.float32))
        norm_own[0, i * rows:(i + 1) * rows, :] = jnp.broadcast_to(
            jnp.sum(acc, axis=1, keepdims=True), (rows, 128)
        )
    norm_b[f] = norm_own[0]
    exchange(lambda k: norm_own.at[0], norm_b, f, in_plane, f_order, 0)
    drain(norm_b, small_recv.at[0], nf - 1)
    norm_c[b] = jnp.sum(norm_b[...], axis=0)
    norm_own[1] = norm_c[b]
    exchange(lambda k: norm_own.at[1], norm_c, b, in_column, b_order, 1)
    drain(norm_c, small_recv.at[1], nb - 1)
    norms = norm_c[...]
    noise_norm = norms[:, :rows, :].reshape(total, 128)[:, :1]
    data_norm = norms[:, rows:, :].reshape(total, 128)
    data_norm = jnp.transpose(data_norm)[:1, :]

    drain(noise_buf, recv_sem.at[0], nb - 1)
    drain(data_buf, recv_sem.at[1], nb - 1)
    acc = jnp.zeros((total, total), jnp.float32)
    chunk = min(1024, w)
    for q in range(w // chunk):
        columns = pl.ds(q * chunk, chunk)
        left = noise_buf[:, :, columns].astype(jnp.float32).reshape(total, chunk).astype(jnp.bfloat16)
        right = data_buf[:, :, columns].astype(jnp.float32).reshape(total, chunk).astype(jnp.bfloat16)
        full[:, columns] = right
        acc = acc + lax.dot_general(
            left, right, (((1,), (1,)), ((), ())), preferred_element_type=jnp.float32
        )
    part[...] = acc.reshape(nb, rows, total)

    a_buf[b] = part[b]
    exchange(lambda k: part.at[lax.rem(b + k, nb)], a_buf, b, in_column, b_order, 2)
    drain(a_buf, small_recv.at[2], nb - 1)
    own[0] = jnp.sum(a_buf[...], axis=0)
    b_buf[f] = own[0]
    exchange(lambda k: own.at[0], b_buf, f, in_plane, f_order, 3)
    drain(b_buf, small_recv.at[3], nf - 1)
    own[1] = jnp.sum(b_buf[...], axis=0)
    c_buf[b] = own[1]
    exchange(lambda k: own.at[1], c_buf, b, in_column, b_order, 4)
    drain(c_buf, small_recv.at[4], nb - 1)
    cross = c_buf[...].reshape(total, total)

    scores = (2.0 * cross - noise_norm - data_norm) / root + 2.0 * root
    column = jnp.zeros((1, total), jnp.float32)
    for _ in range(ITERS):
        row = -log_count - lse(scores + column, 1)
        column = -log_count - lse(scores + row, 0)
    plan = jnp.exp(scores + row + column)
    weights = (plan / jnp.sum(plan, axis=1, keepdims=True)).astype(jnp.bfloat16)

    col_out[...] = column
    pot[...] = jnp.broadcast_to(row, (total, 128)).reshape(nb, rows, 128)
    diagonal = lax.broadcasted_iota(jnp.int32, (rows, 128), 0) == lax.broadcasted_iota(
        jnp.int32, (rows, 128), 1
    )
    flat = jnp.sum(jnp.where(diagonal, pot[b], 0.0), axis=0, keepdims=True)
    row_out[...] = flat[:, :rows]

    groups = 2
    gw = w // groups
    for g in range(groups):
        step = min(512, gw)
        for q in range(gw // step):
            columns = pl.ds(g * gw + q * step, step)
            summed = jnp.dot(weights, full[:, columns], preferred_element_type=jnp.float32)
            obuf[g, :, :, q * step:(q + 1) * step] = summed.reshape(nb, rows, step).astype(jnp.bfloat16)
        here = pl.ds(pl.multiple_of(b * w + g * gw, gw), gw)
        for k in b_order:
            pltpu.make_async_remote_copy(
                src_ref=obuf.at[g, lax.rem(b + k, nb)], dst_ref=out.at[:, here],
                send_sem=out_send.at[g], recv_sem=out_recv.at[g], **in_column(k)
            ).start()
        pltpu.make_async_copy(obuf.at[g, b], out.at[:, here], local_sem.at[g]).start()

    drain(noise_buf, send_sem.at[0], nb - 1)
    drain(data_buf, send_sem.at[1], nb - 1)
    drain(norm_b, small_send.at[0], nf - 1)
    drain(norm_c, small_send.at[1], nb - 1)
    drain(a_buf, small_send.at[2], nb - 1)
    drain(b_buf, small_send.at[3], nf - 1)
    drain(c_buf, small_send.at[4], nb - 1)
    for g in range(groups):
        drain(obuf.at[g], out_send.at[g], nb - 1)
        drain(obuf.at[g], out_recv.at[g], nb - 1)
        pltpu.make_async_copy(
            obuf.at[g, b], out.at[:, pl.ds(pl.multiple_of(b * w + g * gw, gw), gw)], local_sem.at[g]
        ).wait()


def solution(mesh):
    nb, nf = mesh.shape["batch"], mesh.shape["feat"]

    def per_device(noise, data):
        rows, width = noise.shape
        total, w = rows * nb, width // nb
        targets, row, column = pl.pallas_call(
            functools.partial(kernel, nb, nf),
            out_shape=(
                jax.ShapeDtypeStruct((rows, width), jnp.bfloat16),
                jax.ShapeDtypeStruct((1, rows), jnp.float32),
                jax.ShapeDtypeStruct((1, total), jnp.float32),
            ),
            in_specs=[pl.BlockSpec(memory_space=pl.ANY)] * 2,
            out_specs=(
                pl.BlockSpec(memory_space=pl.ANY),
                pl.BlockSpec(memory_space=pltpu.VMEM),
                pl.BlockSpec(memory_space=pltpu.VMEM),
            ),
            scratch_shapes=[
                pltpu.VMEM((nb, rows, w), jnp.bfloat16),
                pltpu.VMEM((nb, rows, w), jnp.bfloat16),
                pltpu.VMEM((2, rows, width), jnp.bfloat16),
                pltpu.VMEM((total, w), jnp.bfloat16),
                pltpu.VMEM((2, nb, rows, w // 2), jnp.bfloat16),
                pltpu.VMEM((nb, rows, total), jnp.float32),
                pltpu.VMEM((2, rows, total), jnp.float32),
                pltpu.VMEM((nb, rows, total), jnp.float32),
                pltpu.VMEM((nf, rows, total), jnp.float32),
                pltpu.VMEM((nb, rows, total), jnp.float32),
                pltpu.VMEM((2, 2 * rows, 128), jnp.float32),
                pltpu.VMEM((nf, 2 * rows, 128), jnp.float32),
                pltpu.VMEM((nb, 2 * rows, 128), jnp.float32),
                pltpu.VMEM((nb, rows, 128), jnp.float32),
                pltpu.SemaphoreType.DMA((4,)),
                pltpu.SemaphoreType.DMA((2,)),
                pltpu.SemaphoreType.DMA((2,)),
                pltpu.SemaphoreType.DMA((5,)),
                pltpu.SemaphoreType.DMA((5,)),
                pltpu.SemaphoreType.DMA((2,)),
                pltpu.SemaphoreType.DMA((2,)),
            ],
            compiler_params=pltpu.CompilerParams(
                collective_id=0, has_side_effects=True, vmem_limit_bytes=56 * 2**20
            ),
        )(noise, data)
        return targets, row.reshape(rows), column.reshape(total)

    return jax.shard_map(
        per_device,
        mesh=mesh,
        in_specs=(P("batch", "feat"), P("batch", "feat")),
        out_specs=(P("batch", "feat"), P("batch"), P()),
        check_vma=False,
    )
```

time: 324 us -> 107 us (0.33)
  blocking collectives: 182 us -> 0 us
  Pallas kernels: 0 us -> 103 us
  waiting for transfers between devices: 100 us -> 0 us
  matrix products: 17.1 us -> 0 us
  between operations: 14.1 us -> 0.65 us
  other arithmetic: 10.8 us -> 0 us
  local copies, waits for them, and re-layouts: 0.01 us -> 3.35 us
    psum x4 -> x0, blocking collectives: 104 us -> none  [the longest x3 70.6 us: per_device(): total = lax.psum(jnp.sum(jnp.exp(shifted - top[None, :]), axis=0), 'batch')]
    pallas_call x0 -> x1, Pallas kernels: none -> 103 us  [per_device(): pl.pallas_call(functools.partial(kernel, nb, nf), out_shape=(jax.ShapeDty...]
    all_gather x1 -> x0, waiting for transfers between devices: 99.7 us -> none  [per_device(): gathered = lax.all_gather(data, 'batch', axis=0, tiled=True)]
    pmax x3 -> x0, blocking collectives: 77.4 us -> none  [per_device(): top = lax.pmax(local_top, 'batch')]
    dot_general x2 -> x0, matrix products: 17.1 us -> none  [the longest x1 9.09 us: per_device(): summed = jnp.dot(weights, gathered, preferred_element_type=jnp.float32)]
    reduce_sum x9 -> x0, other arithmetic: 10.1 us -> none  [the longest x1 7.19 us: per_device(): data_norm = jnp.sum(jnp.square(gathered.astype(jnp.float32)), axis=1)]
    unnamed x6 -> x7, local copies, waits for them, and re-layouts: 0.01 us -> 3.35 us
  transfers between devices with their start and end apart: 1 -> 0, of which waited for: 1 -> 0; matrix products, arithmetic and copies ran while one was open for 1% -> 0% of each run, Pallas kernels for 0% -> 0%
where the time goes in v1:
time: 107 us
  Pallas kernels  103 us (96%)
  local copies, waits for them, and re-layouts  3.35 us (3%)
    pallas_call x1, Pallas kernels, per_device(): pl.pallas_call(functools.partial(kernel, nb, nf), out_shape=(jax.ShapeDty...  103 us
    unnamed x7, local copies, waits for them, and re-layouts  3.35 us

profile of v1, /device:TPU:1, one launch (start us, length us, event | category | flops | bytes accessed | tf_op | source)
XLA Modules:
  0.0 107.3 jit_solution(1224290074271737128)
XLA Ops:
  0.6 103.3 %shard_map.49 = (bf16[8,65536]{1,0:T(8,128)(2,1)}, f32[1,8]{1,0:T(1,128)}, f32[1,128]{1,0:T(1,128)}) custom-call(bf16[8,65536]{1,0:T(8,128)(2,1)} %noise.1, bf16[8,65536]{1,0:T(8,128)(2,1)} %data.1), custom_call_target="tpu_custom_call" | custom-call | tf_op jit(solution)/shard_map/pallas_call | solution.py:188
  103.9 0.0 copy-start.1
  103.9 2.3 %copy.8 = bf16[8,65536]{1,0:T(8,128)(2,1)} copy(bf16[8,65536]{1,0:T(8,128)(2,1)} %get-tuple-element.12) | data formatting | bytes 2097152
  106.2 0.0 copy-done.1
  106.2 0.0 copy-start
  106.2 0.5 copy.9
  106.7 0.1 copy-done
  106.8 0.5 copy.10
Async XLA Ops:
  103.9 2.3 %copy-start.1 = (f32[1,8]{1,0:T(1,128)S(1)}, f32[1,8]{1,0:T(1,128)}, u32[]{:S(2)}) copy-start(f32[1,8]{1,0:T(1,128)} %get-tuple-element.7) | copy-start | bytes 100
  106.2 0.6 copy-start

commit v2 on v1

v2 whole, which is shorter than its diff:
```python
import functools
import math

import jax
import jax.numpy as jnp
from jax import lax
from jax.experimental import pallas as pl
from jax.experimental.pallas import tpu as pltpu
from jax.sharding import PartitionSpec as P

ITERS = 3
SHARED = 6
EARLY = 3
MESH = pl.DeviceIdType.MESH


def lse(values, axis):
    top = jnp.max(values, axis=axis, keepdims=True)
    return top + jnp.log(jnp.sum(jnp.exp(values - top), axis=axis, keepdims=True))


def far_first(count):
    return sorted(range(1, count), key=lambda k: (-min(k, count - k), k))


def kernel(
    nb, nf, noise, data, out, row_out, col_out,
    noise_buf, data_buf, outer_buf, full, outer_full, local_buf, obuf, outer_obuf, part, a_buf, own, b_buf, done, c_buf,
    norm_own, norm_b, pot, wbuf,
    local_sem, outer_send, outer_recv, first_send, first_recv, noise_send, noise_recv, on_send, on_recv,
    small_send, small_recv, out_send, out_recv,
):
    rows, width = noise.shape
    w = width // nb
    total = rows * nb
    piece = total // nf
    features = width * nf
    root = math.sqrt(features)
    log_count = math.log(total)
    half = nb // 4
    shared = w * SHARED // 8
    b, f = lax.axis_index("batch"), lax.axis_index("feat")
    core = lax.rem(b, 2)
    sibling = b + 1 - 2 * core
    b_order, f_order = far_first(nb), list(range(1, nf))

    def at(t):
        return dict(device_id=(t, f), device_id_type=MESH)

    def in_column(k):
        return at(lax.rem(b + k, nb))

    def in_plane(k):
        return dict(device_id=(b, lax.rem(f + k, nf)), device_id_type=MESH)

    def drain(ref, sem, count):
        view = ref.at[pl.ds(0, count)]
        pltpu.make_async_copy(view, view, sem).wait()

    def wrap(t):
        return lax.rem(t + 2 * nb, nb)

    def columns_of(slice_at, q=0, n=w):
        return pl.ds(pl.multiple_of(slice_at * w + q, math.gcd(w, q)), n)

    def step_of(role):
        return 2 if role == 0 else -2

    barrier = pltpu.get_barrier_semaphore()
    for k in b_order:
        pl.semaphore_signal(barrier, inc=1, **in_column(k))
    for k in f_order:
        pl.semaphore_signal(barrier, inc=1, **in_plane(k))
    pl.semaphore_wait(barrier, nb + nf - 2)

    def slice_for(role, member):
        return wrap(member - 2 * role)

    for role in range(2):
        for member in (b, sibling):
            pltpu.make_async_remote_copy(
                src_ref=data.at[:, columns_of(slice_for(role, member))], dst_ref=data_buf.at[1 - role, b],
                send_sem=on_send.at[role, 0], recv_sem=on_recv.at[1 - role, 0],
                **at(wrap(member + step_of(role)))
            ).start()
    for d in range(half - 1, -1, -1):
        for role in range(2):
            for member in ([wrap(sibling + step_of(role) * d)] if d == 0 else []) + (
                [wrap(b + step_of(role) * d), wrap(sibling + step_of(role) * d)] if d else []
            ):
                pltpu.make_async_remote_copy(
                    src_ref=data.at[:, columns_of(slice_for(role, member))], dst_ref=data_buf.at[role, b],
                    send_sem=first_send.at[role, d], recv_sem=first_recv.at[role, d], **at(member)
                ).start()
    locals_ = []
    for role in range(2):
        s = columns_of(slice_for(role, b))
        locals_.append(pltpu.make_async_copy(data.at[:, s], data_buf.at[role, b], local_sem.at[role]))
        locals_.append(pltpu.make_async_copy(noise.at[:, s], noise_buf.at[role, core], local_sem.at[2 + role]))
    locals_.append(pltpu.make_async_copy(noise, local_buf.at[0], local_sem.at[4]))
    locals_.append(pltpu.make_async_copy(data, local_buf.at[1], local_sem.at[5]))
    def outer_slice(role, device):
        return slice_for(role, wrap(device + step_of(role)))

    for role in range(2):
        s = columns_of(outer_slice(role, b), 0, shared)
        locals_.append(pltpu.make_async_copy(data.at[:, s], outer_buf.at[role, b], local_sem.at[6 + role]))
    for c in locals_:
        c.start()
    for role in range(2):
        pltpu.make_async_remote_copy(
            src_ref=data.at[:, columns_of(outer_slice(role, sibling), 0, shared)],
            dst_ref=outer_buf.at[role, b],
            send_sem=outer_send.at[role, 0], recv_sem=outer_recv.at[role, 0], **at(sibling)
        ).start()
    for d in range(half - 1, -1, -1):
        for role in range(2):
            for member in [sibling] if d == 0 else [
                wrap(b + step_of(role) * d), wrap(sibling + step_of(role) * d)
            ]:
                pltpu.make_async_remote_copy(
                    src_ref=noise.at[:, columns_of(slice_for(role, member))],
                    dst_ref=noise_buf.at[role, 2 * d + core],
                    send_sem=noise_send.at[role], recv_sem=noise_recv.at[role], **at(member)
                ).start()
    for c in locals_:
        c.wait()

    def exchange(src_of, buf, slot, partner, order, sem):
        for k in order:
            pltpu.make_async_remote_copy(
                src_ref=src_of(k), dst_ref=buf.at[slot],
                send_sem=small_send.at[sem], recv_sem=small_recv.at[sem], **partner(k)
            ).start()

    chunk = min(2048, width)
    sums = []
    for i in range(2):
        def add(step, acc, i=i):
            v = local_buf[i, :, pl.ds(pl.multiple_of(step * chunk, chunk), chunk)].astype(jnp.float32)
            v = v * v
            for q in range(chunk // 128):
                acc = acc + v[:, q * 128:(q + 1) * 128]
            return acc
        acc = lax.fori_loop(0, width // chunk, add, jnp.zeros((rows, 128), jnp.float32))
        sums.append(jnp.sum(acc, axis=1, keepdims=True))
    lane = lax.broadcasted_iota(jnp.int32, (rows, 128), 1)
    norm_own[...] = jnp.where(lane < 64, sums[0], sums[1])
    norm_b[f] = norm_own[...]
    exchange(lambda k: norm_own, norm_b, f, in_plane, f_order, 0)

    def pair(chip_of):
        return pl.ds(pl.multiple_of(wrap(chip_of) // 2 * 2, 2), 2)

    for d in range(half - 1, 0, -1):
        for role in range(2):
            drain(data_buf.at[role], first_recv.at[role, d], 2)
            block = pair(b - step_of(role) * d)
            pltpu.make_async_remote_copy(
                src_ref=data_buf.at[role, block], dst_ref=data_buf.at[1 - role, block],
                send_sem=on_send.at[role, d], recv_sem=on_recv.at[1 - role, d],
                **at(wrap(b + step_of(role)))
            ).start()
    for role in range(2):
        drain(data_buf.at[role], first_recv.at[role, 0], 1)

    drain(norm_b, small_recv.at[0], nf - 1)
    own[piece:, :] = jnp.sum(norm_b[...], axis=0)

    for role in range(2):
        drain(noise_buf.at[role], noise_recv.at[role], nb // 2 - 1)
    for d in range(half):
        for role in range(2):
            drain(data_buf.at[role], on_recv.at[role, d], 2)

    def share(offsets):
        for d in offsets:
            for role in range(2):
                block = pair(b + step_of(role) * d)
                pltpu.make_async_remote_copy(
                    src_ref=data_buf.at[role, block, :, pl.ds(0, shared)], dst_ref=outer_buf.at[role, block],
                    send_sem=outer_send.at[role, 1], recv_sem=outer_recv.at[role, 1],
                    **at(wrap(b - step_of(role)))
                ).start()

    onward = list(range(nb // 2 - 1))
    share(onward[:EARLY])

    acc = jnp.zeros((total, total), jnp.float32)
    chunk = min(1024, w)
    served = total // 2
    for q in range(w // chunk):
        columns = pl.ds(q * chunk, chunk)
        for role in range(2):
            left = data_buf[role, :, :, columns].astype(jnp.float32).reshape(total, chunk).astype(jnp.bfloat16)
            right = noise_buf[role, :, :, columns].astype(jnp.float32).reshape(served, chunk).astype(jnp.bfloat16)
            zero = jnp.zeros((served, chunk), jnp.bfloat16)
            right = jnp.concatenate([right, zero] if role == 0 else [zero, right], axis=0)
            acc = acc + lax.dot_general(
                left, right, (((1,), (1,)), ((), ())), preferred_element_type=jnp.float32
            )
    part[...] = acc.reshape(nf, total // nf, total)

    a_buf[f] = part[f]
    exchange(lambda k: part.at[lax.rem(f + k, nf)], a_buf, f, in_plane, f_order, 1)
    drain(a_buf, small_recv.at[1], nf - 1)
    mine = jnp.sum(a_buf[...], axis=0)
    lane = lax.broadcasted_iota(jnp.int32, mine.shape, 1)
    spread = jnp.zeros_like(mine)
    for d in range(half):
        for role in range(2):
            at_lane = role * served + d * 2 * rows
            chip = wrap(b - core - step_of(role) * d)
            group = jnp.where((lane >= at_lane) & (lane < at_lane + 2 * rows), mine, 0.0)
            spread = spread + pltpu.roll(group, lax.rem(chip * rows - at_lane + total, total), 1)
    own[:piece, :] = spread
    b_buf[b] = own[...]
    exchange(lambda k: own, b_buf, b, in_column, b_order, 2)
    share(onward[EARLY:])
    for role in range(2):
        for q in range(w // chunk):
            columns = pl.ds(q * chunk, chunk)
            full[role, :, columns] = (
                data_buf[role, :, :, columns].astype(jnp.float32).reshape(total, chunk).astype(jnp.bfloat16)
            )
    drain(b_buf, small_recv.at[2], nb - 1)
    done[...] = jnp.sum(b_buf[:, :piece, :], axis=0)
    c_buf[f] = done[...]
    exchange(lambda k: done, c_buf, f, in_plane, f_order, 3)
    norms = b_buf[:, piece:, :].reshape(total, 128)
    noise_norm = norms[:, :1]
    data_norm = jnp.transpose(norms)[64:65, :]
    drain(c_buf, small_recv.at[3], nf - 1)
    cross = jnp.transpose(c_buf[...].reshape(total, total))

    scores = (2.0 * cross - noise_norm - data_norm) / root + 2.0 * root
    column = jnp.zeros((1, total), jnp.float32)
    for _ in range(ITERS):
        row = -log_count - lse(scores + column, 1)
        column = -log_count - lse(scores + row, 0)
    plan = jnp.exp(scores + row + column)
    weights = plan / jnp.sum(plan, axis=1, keepdims=True)
    wbuf[...] = weights.reshape(nb, rows, total)

    step = min(512, shared)
    kept = []

    def targets(chips, role, values, buf, slice_at, first, count, sem):
        blocks = []
        for d in chips:
            blocks += [wrap(sibling - step_of(role) * d), wrap(b - step_of(role) * d)]
        chosen = jnp.concatenate([wbuf[t] for t in blocks], axis=0).astype(jnp.bfloat16)
        for q in range(0, count, step):
            n = min(step, count - q)
            summed = jnp.dot(chosen, values[role, :, first + q:first + q + n], preferred_element_type=jnp.float32)
            buf[role, :len(blocks), :, first + q:first + q + n] = summed.reshape(
                len(blocks), rows, n
            ).astype(jnp.bfloat16)
        where = columns_of(slice_at, first, count)
        for j, t in enumerate(blocks):
            source = buf.at[role, j, :, pl.ds(first, count)]
            if j == len(blocks) - 1 and chips[-1] == 0:
                c = pltpu.make_async_copy(source, out.at[:, where], local_sem.at[sem])
                c.start()
                kept.append(c)
            else:
                pltpu.make_async_remote_copy(
                    src_ref=source, dst_ref=out.at[:, where],
                    send_sem=out_send.at[sem], recv_sem=out_recv.at[sem], **at(t)
                ).start()

    far = list(range(half - 1, -1, -1))
    for role in range(2):
        targets(far, role, full, obuf, slice_for(role, b), shared, w - shared, role)
    for role in range(2):
        drain(outer_buf.at[role], outer_recv.at[role, 0], 1)
        drain(outer_buf.at[role], outer_recv.at[role, 1], nb - 2)
        for q in range(0, shared, step):
            columns = pl.ds(q, step)
            outer_full[role, :, columns] = (
                outer_buf[role, :, :, columns].astype(jnp.float32).reshape(total, step).astype(jnp.bfloat16)
            )
        targets(far[1:], role, outer_full, outer_obuf, outer_slice(role, b), 0, shared, 2 + role)
    for role in range(2):
        targets([0], role, full, obuf, slice_for(role, b), 0, shared, 4 + role)

    col_out[...] = column
    pot[...] = jnp.broadcast_to(row, (total, 128)).reshape(nb, rows, 128)
    diagonal = lax.broadcasted_iota(jnp.int32, (rows, 128), 0) == lax.broadcasted_iota(
        jnp.int32, (rows, 128), 1
    )
    flat = jnp.sum(jnp.where(diagonal, pot[b], 0.0), axis=0, keepdims=True)
    row_out[...] = flat[:, :rows]

    for role in range(2):
        for d in range(half):
            drain(data_buf.at[role], first_send.at[role, d], 2 if d else 1)
            drain(data_buf.at[role], on_send.at[role, d], 2)
        drain(noise_buf.at[role], noise_send.at[role], nb // 2 - 1)
    drain(norm_b, small_send.at[0], nf - 1)
    drain(a_buf, small_send.at[1], nf - 1)
    drain(b_buf, small_send.at[2], nb - 1)
    drain(c_buf, small_send.at[3], nf - 1)
    for role in range(2):
        drain(outer_buf.at[role], outer_send.at[role, 0], 1)
        drain(outer_buf.at[role], outer_send.at[role, 1], nb - 2)
        for sem, first, count, blocks in (
            (role, shared, w - shared, nb // 2 - 1), (2 + role, 0, shared, nb // 2 - 3), (4 + role, 0, shared, 1)
        ):
            view = obuf.at[role, pl.ds(0, blocks), :, pl.ds(first, count)]
            pltpu.make_async_copy(view, view, out_send.at[sem]).wait()
            pltpu.make_async_copy(view, view, out_recv.at[sem]).wait()
    for c in kept:
        c.wait()


def solution(mesh):
    nb, nf = mesh.shape["batch"], mesh.shape["feat"]

    def per_device(noise, data):
        rows, width = noise.shape
        total, w = rows * nb, width // nb
        piece, shared = total // nf, w * SHARED // 8
        targets, row, column = pl.pallas_call(
            functools.partial(kernel, nb, nf),
            out_shape=(
                jax.ShapeDtypeStruct((rows, width), jnp.bfloat16),
                jax.ShapeDtypeStruct((1, rows), jnp.float32),
                jax.ShapeDtypeStruct((1, total), jnp.float32),
            ),
            in_specs=[pl.BlockSpec(memory_space=pl.ANY)] * 2,
            out_specs=(
                pl.BlockSpec(memory_space=pl.ANY),
                pl.BlockSpec(memory_space=pltpu.VMEM),
                pl.BlockSpec(memory_space=pltpu.VMEM),
            ),
            scratch_shapes=[
                pltpu.VMEM((2, nb // 2, rows, w), jnp.bfloat16),
                pltpu.VMEM((2, nb, rows, w), jnp.bfloat16),
                pltpu.VMEM((2, nb, rows, shared), jnp.bfloat16),
                pltpu.VMEM((2, total, w), jnp.bfloat16),
                pltpu.VMEM((2, total, shared), jnp.bfloat16),
                pltpu.VMEM((2, rows, width), jnp.bfloat16),
                pltpu.VMEM((2, nb // 2, rows, w), jnp.bfloat16),
                pltpu.VMEM((2, nb // 2 - 2, rows, shared), jnp.bfloat16),
                pltpu.VMEM((nf, piece, total), jnp.float32),
                pltpu.VMEM((nf, piece, total), jnp.float32),
                pltpu.VMEM((piece + rows, total), jnp.float32),
                pltpu.VMEM((nb, piece + rows, total), jnp.float32),
                pltpu.VMEM((piece, total), jnp.float32),
                pltpu.VMEM((nf, piece, total), jnp.float32),
                pltpu.VMEM((rows, 128), jnp.float32),
                pltpu.VMEM((nf, rows, 128), jnp.float32),
                pltpu.VMEM((nb, rows, 128), jnp.float32),
                pltpu.VMEM((nb, rows, total), jnp.float32),
                pltpu.SemaphoreType.DMA((8,)),
                pltpu.SemaphoreType.DMA((2, 2)),
                pltpu.SemaphoreType.DMA((2, 2)),
                pltpu.SemaphoreType.DMA((2, nb // 4)),
                pltpu.SemaphoreType.DMA((2, nb // 4)),
                pltpu.SemaphoreType.DMA((2,)),
                pltpu.SemaphoreType.DMA((2,)),
                pltpu.SemaphoreType.DMA((2, nb // 4)),
                pltpu.SemaphoreType.DMA((2, nb // 4)),
                pltpu.SemaphoreType.DMA((4,)),
                pltpu.SemaphoreType.DMA((4,)),
                pltpu.SemaphoreType.DMA((6,)),
                pltpu.SemaphoreType.DMA((6,)),
            ],
            compiler_params=pltpu.CompilerParams(
                collective_id=0, has_side_effects=True, vmem_limit_bytes=56 * 2**20
            ),
        )(noise, data)
        return targets, row.reshape(rows), column.reshape(total)

    return jax.shard_map(
        per_device,
        mesh=mesh,
        in_specs=(P("batch", "feat"), P("batch", "feat")),
        out_specs=(P("batch", "feat"), P("batch"), P()),
        check_vma=False,
    )
```

time: 107 us -> 93.4 us (0.87)
  Pallas kernels: 103 us -> 89.2 us
    pallas_call x1, Pallas kernels: 103 us -> 89.2 us  [per_device(): pl.pallas_call(functools.partial(kernel, nb, nf), out_shape=(jax.ShapeDty...]
where the time goes in v2:
time: 93.4 us; the launch traced here: 93.3 us
  Pallas kernels  89.2 us (96%)
  local copies, waits for them, and re-layouts  3.35 us (4%)
    pallas_call x1, Pallas kernels, per_device(): pl.pallas_call(functools.partial(kernel, nb, nf), out_shape=(jax.ShapeDty...  89.2 us
    unnamed x7, local copies, waits for them, and re-layouts  3.35 us

profile of v2, /device:TPU:1, one launch (start us, length us, event | category | flops | bytes accessed | tf_op | source)
XLA Modules:
  0.0 93.3 jit_solution(17576534574252647715)
XLA Ops:
  0.6 89.2 %shard_map.49 = (bf16[8,65536]{1,0:T(8,128)(2,1)}, f32[1,8]{1,0:T(1,128)}, f32[1,128]{1,0:T(1,128)}) custom-call(bf16[8,65536]{1,0:T(8,128)(2,1)} %noise.1, bf16[8,65536]{1,0:T(8,128)(2,1)} %data.1), custom_call_target="tpu_custom_call" | custom-call | tf_op jit(solution)/shard_map/pallas_call | solution.py:324
  89.9 0.0 copy-start.1
  89.9 2.3 %copy.8 = bf16[8,65536]{1,0:T(8,128)(2,1)} copy(bf16[8,65536]{1,0:T(8,128)(2,1)} %get-tuple-element.12) | data formatting | bytes 2097152
  92.2 0.0 copy-done.1
  92.2 0.0 copy-start
  92.2 0.5 copy.9
  92.7 0.1 copy-done
  92.7 0.5 copy.10
Async XLA Ops:
  89.9 2.3 %copy-start.1 = (f32[1,8]{1,0:T(1,128)S(1)}, f32[1,8]{1,0:T(1,128)}, u32[]{:S(2)}) copy-start(f32[1,8]{1,0:T(1,128)} %get-tuple-element.7) | copy-start | bytes 100
  92.2 0.6 copy-start

commit v3 on v2

--- a/solution.py
+++ b/solution.py
@@ -26,14 +26,13 @@
 def kernel(
     nb, nf, noise, data, out, row_out, col_out,
     noise_buf, data_buf, outer_buf, full, outer_full, local_buf, obuf, outer_obuf, part, a_buf, own, b_buf, done, c_buf,
-    norm_own, norm_b, pot, wbuf,
+    norm_own, norm_own2, norm_b, pot, wbuf,
     local_sem, outer_send, outer_recv, first_send, first_recv, noise_send, noise_recv, on_send, on_recv,
     small_send, small_recv, out_send, out_recv,
 ):
     rows, width = noise.shape
     w = width // nb
     total = rows * nb
-    piece = total // nf
     features = width * nf
     root = math.sqrt(features)
     log_count = math.log(total)
@@ -165,7 +164,11 @@
         drain(data_buf.at[role], first_recv.at[role, 0], 1)
 
     drain(norm_b, small_recv.at[0], nf - 1)
-    own[piece:, :] = jnp.sum(norm_b[...], axis=0)
+    norms = jnp.sum(norm_b[...], axis=0)
+    diagonal = lax.broadcasted_iota(jnp.int32, (rows, 128), 0) == lane
+    along = jnp.sum(jnp.where(diagonal, norms[:, 64:65], 0.0), axis=0, keepdims=True)
+    along = pltpu.roll(jnp.broadcast_to(along, (rows, 128)), b * rows, 1)
+    norm_own2[...] = -along - jnp.where(b == f, norms[:, :1], 0.0)
 
     for role in range(2):
         drain(noise_buf.at[role], noise_recv.at[role], nb // 2 - 1)
@@ -186,34 +189,30 @@
     onward = list(range(nb // 2 - 1))
     share(onward[:EARLY])
 
-    acc = jnp.zeros((total, total), jnp.float32)
     chunk = min(1024, w)
     served = total // 2
-    for q in range(w // chunk):
-        columns = pl.ds(q * chunk, chunk)
-        for role in range(2):
-            left = data_buf[role, :, :, columns].astype(jnp.float32).reshape(total, chunk).astype(jnp.bfloat16)
-            right = noise_buf[role, :, :, columns].astype(jnp.float32).reshape(served, chunk).astype(jnp.bfloat16)
-            zero = jnp.zeros((served, chunk), jnp.bfloat16)
-            right = jnp.concatenate([right, zero] if role == 0 else [zero, right], axis=0)
+    for role in range(2):
+        acc = jnp.zeros((served, total), jnp.float32)
+        for q in range(w // chunk):
+            columns = pl.ds(q * chunk, chunk)
+            left = noise_buf[role, :, :, columns].astype(jnp.float32).reshape(served, chunk).astype(jnp.bfloat16)
+            right = data_buf[role, :, :, columns].astype(jnp.float32).reshape(total, chunk).astype(jnp.bfloat16)
             acc = acc + lax.dot_general(
                 left, right, (((1,), (1,)), ((), ())), preferred_element_type=jnp.float32
             )
-    part[...] = acc.reshape(nf, total // nf, total)
+        acc = acc.reshape(half, 2, rows, total)
+        for d in range(half):
+            block = pair(b - step_of(role) * d)
+            if role and not d:
+                part[block] = part[block] + acc[d]
+            else:
+                part[block] = acc[d]
+    part[pair(b + nb // 2)] = jnp.zeros((2, rows, total), jnp.float32)
 
     a_buf[f] = part[f]
     exchange(lambda k: part.at[lax.rem(f + k, nf)], a_buf, f, in_plane, f_order, 1)
     drain(a_buf, small_recv.at[1], nf - 1)
-    mine = jnp.sum(a_buf[...], axis=0)
-    lane = lax.broadcasted_iota(jnp.int32, mine.shape, 1)
-    spread = jnp.zeros_like(mine)
-    for d in range(half):
-        for role in range(2):
-            at_lane = role * served + d * 2 * rows
-            chip = wrap(b - core - step_of(role) * d)
-            group = jnp.where((lane >= at_lane) & (lane < at_lane + 2 * rows), mine, 0.0)
-            spread = spread + pltpu.roll(group, lax.rem(chip * rows - at_lane + total, total), 1)
-    own[:piece, :] = spread
+    own[...] = 2.0 * jnp.sum(a_buf[...], axis=0) + norm_own2[...]
     b_buf[b] = own[...]
     exchange(lambda k: own, b_buf, b, in_column, b_order, 2)
     share(onward[EARLY:])
@@ -224,16 +223,11 @@
                 data_buf[role, :, :, columns].astype(jnp.float32).reshape(total, chunk).astype(jnp.bfloat16)
             )
     drain(b_buf, small_recv.at[2], nb - 1)
-    done[...] = jnp.sum(b_buf[:, :piece, :], axis=0)
+    done[...] = jnp.sum(b_buf[...], axis=0)
     c_buf[f] = done[...]
     exchange(lambda k: done, c_buf, f, in_plane, f_order, 3)
-    norms = b_buf[:, piece:, :].reshape(total, 128)
-    noise_norm = norms[:, :1]
-    data_norm = jnp.transpose(norms)[64:65, :]
     drain(c_buf, small_recv.at[3], nf - 1)
-    cross = jnp.transpose(c_buf[...].reshape(total, total))
-
-    scores = (2.0 * cross - noise_norm - data_norm) / root + 2.0 * root
+    scores = c_buf[...].reshape(total, total) / root + 2.0 * root
     column = jnp.zeros((1, total), jnp.float32)
     for _ in range(ITERS):
         row = -log_count - lse(scores + column, 1)
@@ -242,10 +236,10 @@
     weights = plan / jnp.sum(plan, axis=1, keepdims=True)
     wbuf[...] = weights.reshape(nb, rows, total)
 
-    step = min(512, shared)
+    step = math.gcd(512, shared)
     kept = []
 
-    def targets(chips, role, values, buf, slice_at, first, count, sem):
+    def targets(chips, role, values, buf, first, count):
         blocks = []
         for d in chips:
             blocks += [wrap(sibling - step_of(role) * d), wrap(b - step_of(role) * d)]
@@ -256,22 +250,44 @@
             buf[role, :len(blocks), :, first + q:first + q + n] = summed.reshape(
                 len(blocks), rows, n
             ).astype(jnp.bfloat16)
+
+    def to_device(source, where, t, sem):
+        pltpu.make_async_remote_copy(
+            src_ref=source, dst_ref=out.at[:, where],
+            send_sem=out_send.at[sem], recv_sem=out_recv.at[sem], **at(t)
+        ).start()
+
+    def to_own(buf, role, place, slice_at, first, count, sem):
         where = columns_of(slice_at, first, count)
-        for j, t in enumerate(blocks):
-            source = buf.at[role, j, :, pl.ds(first, count)]
-            if j == len(blocks) - 1 and chips[-1] == 0:
-                c = pltpu.make_async_copy(source, out.at[:, where], local_sem.at[sem])
-                c.start()
-                kept.append(c)
-            else:
-                pltpu.make_async_remote_copy(
-                    src_ref=source, dst_ref=out.at[:, where],
-                    send_sem=out_send.at[sem], recv_sem=out_recv.at[sem], **at(t)
-                ).start()
+        to_device(buf.at[role, place, :, pl.ds(first, count)], where, sibling, sem)
+        c = pltpu.make_async_copy(
+            buf.at[role, place + 1, :, pl.ds(first, count)], out.at[:, where], local_sem.at[sem]
+        )
+        c.start()
+        kept.append(c)
+
+    def to_chips(chips, buf, slice_of, first, count, sem, wanted):
+        for q in wanted:
+            for role in range(2):
+                d = lax.rem((b // 2 - q if role == 0 else q - b // 2) + nb, nb // 2)
+
+                @pl.when((d >= max(chips[-1], 1)) & (d <= chips[0]))
+                def _(q=q, role=role, d=d):
+                    where = columns_of(slice_of(role, b), first, count)
+                    for i, t in enumerate((2 * q + 1 - core, 2 * q + core)):
+                        place = 2 * (chips[0] - d) + i
+                        to_device(buf.at[role, place, :, pl.ds(first, count)], where, t, sem + role)
 
     far = list(range(half - 1, -1, -1))
-    for role in range(2):
-        targets(far, role, full, obuf, slice_for(role, b), shared, w - shared, role)
+    low, high = range(nb // 4), range(nb // 4, nb // 2)
+    inner = (far, obuf, slice_for, shared, w - shared, 0)
+    outer = (far[1:], outer_obuf, outer_slice, 0, shared, 2)
+    for role in range(2):
+        targets(far, role, full, obuf, shared, w - shared)
+    to_chips(*inner, low)
+    to_chips(*inner, high)
+    for role in range(2):
+        to_own(obuf, role, nb // 2 - 2, slice_for(role, b), shared, w - shared, role)
     for role in range(2):
         drain(outer_buf.at[role], outer_recv.at[role, 0], 1)
         drain(outer_buf.at[role], outer_recv.at[role, 1], nb - 2)
@@ -280,15 +296,17 @@
             outer_full[role, :, columns] = (
                 outer_buf[role, :, :, columns].astype(jnp.float32).reshape(total, step).astype(jnp.bfloat16)
             )
-        targets(far[1:], role, outer_full, outer_obuf, outer_slice(role, b), 0, shared, 2 + role)
-    for role in range(2):
-        targets([0], role, full, obuf, slice_for(role, b), 0, shared, 4 + role)
+        targets(far[1:], role, outer_full, outer_obuf, 0, shared)
+    to_chips(*outer, low)
+    for role in range(2):
+        to_own(outer_obuf, role, nb // 2 - 4, outer_slice(role, b), 0, shared, 2 + role)
+    for role in range(2):
+        targets([0], role, full, obuf, 0, shared)
+        to_own(obuf, role, 0, slice_for(role, b), 0, shared, 4 + role)
+    to_chips(*outer, high)
 
     col_out[...] = column
     pot[...] = jnp.broadcast_to(row, (total, 128)).reshape(nb, rows, 128)
-    diagonal = lax.broadcasted_iota(jnp.int32, (rows, 128), 0) == lax.broadcasted_iota(
-        jnp.int32, (rows, 128), 1
-    )
     flat = jnp.sum(jnp.where(diagonal, pot[b], 0.0), axis=0, keepdims=True)
     row_out[...] = flat[:, :rows]
 
@@ -330,7 +348,7 @@
             ),
             in_specs=[pl.BlockSpec(memory_space=pl.ANY)] * 2,
             out_specs=(
-                pl.BlockSpec(memory_space=pl.ANY),
+                pl.BlockSpec(memory_space=pltpu.VMEM),
                 pl.BlockSpec(memory_space=pltpu.VMEM),
                 pl.BlockSpec(memory_space=pltpu.VMEM),
             ),
@@ -345,10 +363,11 @@
                 pltpu.VMEM((2, nb // 2 - 2, rows, shared), jnp.bfloat16),
                 pltpu.VMEM((nf, piece, total), jnp.float32),
                 pltpu.VMEM((nf, piece, total), jnp.float32),
-                pltpu.VMEM((piece + rows, total), jnp.float32),
-                pltpu.VMEM((nb, piece + rows, total), jnp.float32),
+                pltpu.VMEM((piece, total), jnp.float32),
+                pltpu.VMEM((nb, piece, total), jnp.float32),
                 pltpu.VMEM((piece, total), jnp.float32),
                 pltpu.VMEM((nf, piece, total), jnp.float32),
+                pltpu.VMEM((rows, 128), jnp.float32),
                 pltpu.VMEM((rows, 128), jnp.float32),
                 pltpu.VMEM((nf, rows, 128), jnp.float32),
                 pltpu.VMEM((nb, rows, 128), jnp.float32),
@@ -368,7 +387,7 @@
                 pltpu.SemaphoreType.DMA((6,)),
             ],
             compiler_params=pltpu.CompilerParams(
-                collective_id=0, has_side_effects=True, vmem_limit_bytes=56 * 2**20
+                collective_id=0, has_side_effects=True, vmem_limit_bytes=52 * 2**20
             ),
         )(noise, data)
         return targets, row.reshape(rows), column.reshape(total)

time: 93.4 us -> 89.4 us (0.957); the launches traced: 93.3 us -> 88.1 us
  Pallas kernels: 89.2 us -> 85.4 us
  local copies, waits for them, and re-layouts: 3.35 us -> 1.99 us
    pallas_call x1, Pallas kernels: 89.2 us -> 85.4 us  [per_device(): pl.pallas_call(functools.partial(kernel, nb, nf), out_shape=(jax.ShapeDty...]
    unnamed x7 -> x3, local copies, waits for them, and re-layouts: 3.35 us -> 1.99 us
where the time goes in v3:
time: 89.4 us; the launch traced here: 88.1 us
  Pallas kernels  85.4 us (96%)
  local copies, waits for them, and re-layouts  1.99 us (2%)
    pallas_call x1, Pallas kernels, per_device(): pl.pallas_call(functools.partial(kernel, nb, nf), out_shape=(jax.ShapeDty...  85.4 us
    unnamed x3, local copies, waits for them, and re-layouts  1.99 us

profile of v3, /device:TPU:1, one launch (start us, length us, event | category | flops | bytes accessed | tf_op | source)
XLA Modules:
  0.0 88.1 jit_solution(15894770814420126484)
XLA Ops:
  0.6 85.4 %shard_map.49 = (bf16[8,65536]{1,0:T(8,128)(2,1)S(1)}, f32[1,8]{1,0:T(1,128)S(1)}, f32[1,128]{1,0:T(1,128)S(1)}) custom-call(bf16[8,65536]{1,0:T(8,128)(2,1)} %noise.1, bf16[8,65536]{1,0:T(8,128)(2,1)} %data.1), custom_call_target="tpu_custom_call" | custom-call | tf_op jit(solution)/shard_map/pallas_call | solution.py:342
  86.1 1.0 %copy.8 = bf16[8,65536]{1,0:T(8,128)(2,1)} copy(bf16[8,65536]{1,0:T(8,128)(2,1)S(1)} %get-tuple-element.12) | data formatting | bytes 2097152
  87.0 0.5 copy.9
  87.6 0.5 copy.10

commit v4 on v3

v4 whole, which is shorter than its diff:
```python
import functools
import math

import jax
import jax.numpy as jnp
from jax import lax
from jax.experimental import pallas as pl
from jax.experimental.pallas import tpu as pltpu
from jax.sharding import PartitionSpec as P

ITERS = 3
SHARED = 7
EARLY = 3
MESH = pl.DeviceIdType.MESH


def lse(values, axis):
    top = jnp.max(values, axis=axis, keepdims=True)
    return top + jnp.log(jnp.sum(jnp.exp(values - top), axis=axis, keepdims=True))


def far_first(count):
    return sorted(range(1, count), key=lambda k: (-min(k, count - k), k))


def kernel(
    nb, nf, noise, data, out, row_out, col_out,
    noise_buf, data_buf, outer_buf, full, outer_full, local_buf, obuf, outer_obuf,
    part, a_buf, own, b_buf, done, c_buf, norm_own, norm_b, pot, wbuf,
    local_sem, outer_send, outer_recv, first_send, first_recv, noise_send, noise_recv, on_send, on_recv,
    small_send, small_recv, out_send, out_recv,
):
    rows, width = noise.shape
    w = width // nb
    total = rows * nb
    piece = total // nf
    features = width * nf
    root = math.sqrt(features)
    log_count = math.log(total)
    half = nb // 4
    shared = w * SHARED // 8
    b, f = lax.axis_index("batch"), lax.axis_index("feat")
    core = lax.rem(b, 2)
    sibling = b + 1 - 2 * core
    b_order, f_order = far_first(nb), list(range(1, nf))

    def at(t):
        return dict(device_id=(t, f), device_id_type=MESH)

    def in_column(k):
        return at(lax.rem(b + k, nb))

    def in_plane(k):
        return dict(device_id=(b, lax.rem(f + k, nf)), device_id_type=MESH)

    def drain(ref, sem, count):
        view = ref.at[pl.ds(0, count)]
        pltpu.make_async_copy(view, view, sem).wait()

    def wrap(t):
        return lax.rem(t + 2 * nb, nb)

    def pair(device):
        return pl.ds(pl.multiple_of(wrap(device) // 2 * 2, 2), 2)

    def columns_of(slice_at, q=0, n=w):
        return pl.ds(pl.multiple_of(slice_at * w + q, math.gcd(w, q)), n)

    def step_of(role):
        return 2 if role == 0 else -2

    def slice_for(role, member):
        return wrap(member - 2 * role)

    def outer_slice(role, device):
        return slice_for(role, wrap(device + step_of(role)))

    def remote(source, target, send, recv, device):
        pltpu.make_async_remote_copy(
            src_ref=source, dst_ref=target, send_sem=send, recv_sem=recv, **device
        ).start()

    barrier = pltpu.get_barrier_semaphore()
    for k in b_order:
        pl.semaphore_signal(barrier, inc=1, **in_column(k))
    for k in f_order:
        pl.semaphore_signal(barrier, inc=1, **in_plane(k))
    pl.semaphore_wait(barrier, nb + nf - 2)

    for role in range(2):
        for member in (b, sibling):
            remote(
                data.at[:, columns_of(slice_for(role, member))], data_buf.at[1 - role, b],
                on_send.at[role, 0], on_recv.at[1 - role, 0], at(wrap(member + step_of(role))),
            )
    for d in range(half - 1, -1, -1):
        for role in range(2):
            for member in [sibling] if d == 0 else [
                wrap(b + step_of(role) * d), wrap(sibling + step_of(role) * d)
            ]:
                source = data.at[:, columns_of(slice_for(role, member))]
                if d > 1:
                    remote(
                        source, outer_buf.at[role, b],
                        first_send.at[role, d], outer_recv.at[role, d], at(wrap(member - step_of(role))),
                    )
                else:
                    remote(
                        source, data_buf.at[role, b], first_send.at[role, d], first_recv.at[role, d], at(member)
                    )
    locals_ = []
    for role in range(2):
        s = columns_of(slice_for(role, b))
        locals_.append(pltpu.make_async_copy(data.at[:, s], data_buf.at[role, b], local_sem.at[role]))
        locals_.append(pltpu.make_async_copy(noise.at[:, s], noise_buf.at[role, core], local_sem.at[2 + role]))
        s = columns_of(outer_slice(role, b))
        locals_.append(pltpu.make_async_copy(data.at[:, s], outer_buf.at[role, b], local_sem.at[6 + role]))
    locals_.append(pltpu.make_async_copy(noise, local_buf.at[0], local_sem.at[4]))
    locals_.append(pltpu.make_async_copy(data, local_buf.at[1], local_sem.at[5]))
    for c in locals_:
        c.start()
    for role in range(2):
        remote(
            data.at[:, columns_of(outer_slice(role, sibling))], outer_buf.at[role, b],
            outer_send.at[role, 0], outer_recv.at[role, 0], at(sibling),
        )

    def send_noise(distances):
        for d in distances:
            for role in range(2):
                for member in [sibling] if d == 0 else [
                    wrap(b + step_of(role) * d), wrap(sibling + step_of(role) * d)
                ]:
                    remote(
                        noise.at[:, columns_of(slice_for(role, member))], noise_buf.at[role, 2 * d + core],
                        noise_send.at[role], noise_recv.at[role], at(member),
                    )

    send_noise([half - 1])
    for c in locals_:
        c.wait()

    def exchange(src_of, buf, slot, partner, order, sem):
        for k in order:
            remote(src_of(k), buf.at[slot], small_send.at[sem], small_recv.at[sem], partner(k))

    chunk = min(2048, width)
    sums = []
    for i in range(2):
        def add(step, acc, i=i):
            v = local_buf[i, :, pl.ds(pl.multiple_of(step * chunk, chunk), chunk)].astype(jnp.float32)
            v = v * v
            for q in range(chunk // 128):
                acc = acc + v[:, q * 128:(q + 1) * 128]
            return acc
        acc = lax.fori_loop(0, width // chunk, add, jnp.zeros((rows, 128), jnp.float32))
        sums.append(jnp.sum(acc, axis=1, keepdims=True))
    lane = lax.broadcasted_iota(jnp.int32, (rows, 128), 1)
    sublane = lax.broadcasted_iota(jnp.int32, (rows, 128), 0)
    norm_own[...] = jnp.where(lane < 64, sums[0], sums[1])
    norm_b[f] = norm_own[...]
    exchange(lambda k: norm_own, norm_b, f, in_plane, f_order, 0)

    def onward(d):
        for role in range(2):
            drain(data_buf.at[role], first_recv.at[role, d], 2)
            block = pair(b - step_of(role) * d)
            remote(
                data_buf.at[role, block], data_buf.at[1 - role, block],
                on_send.at[role, d], on_recv.at[1 - role, d], at(wrap(b + step_of(role))),
            )

    for d in range(half - 1, 1, -1):
        for role in range(2):
            drain(outer_buf.at[role], outer_recv.at[role, d], 2)
            block = pair(b - step_of(role) * (d - 1))
            remote(
                outer_buf.at[role, block], data_buf.at[role, block],
                outer_send.at[role, d], first_recv.at[role, d], at(wrap(b + step_of(role))),
            )
    onward(1)
    send_noise(range(half - 2, 1, -1))
    for d in range(half - 1, 1, -1):
        onward(d)
    send_noise([1, 0])

    drain(norm_b, small_recv.at[0], nf - 1)
    norms = jnp.sum(norm_b[...], axis=0)
    picked = jnp.where(lane == sublane, norms[:, :1], jnp.where(lane == sublane + rows, norms[:, 64:65], 0.0))
    own[piece:, :] = jnp.sum(picked, axis=0, keepdims=True)

    for role in range(2):
        drain(data_buf.at[role], first_recv.at[role, 0], 1)
        for d in range(half):
            drain(data_buf.at[role], on_recv.at[role, d], 2)
    def share(offsets):
        for d in offsets:
            for role in range(2):
                block = pair(b + step_of(role) * d)
                remote(
                    data_buf.at[role, block, :, pl.ds(0, shared)], outer_buf.at[role, block, :, pl.ds(0, shared)],
                    outer_send.at[role, 1], outer_recv.at[role, 1], at(wrap(b - step_of(role))),
                )

    offsets = list(range(half + 1))
    share(offsets[:EARLY])

    chunk = min(1024, w)
    for role in range(2):
        for q in range(w // chunk):
            columns = pl.ds(q * chunk, chunk)
            full[role, :, columns] = (
                data_buf[role, :, :, columns].astype(jnp.float32).reshape(total, chunk).astype(jnp.bfloat16)
            )
    for role in range(2):
        drain(noise_buf.at[role], noise_recv.at[role], nb // 2 - 1)

    served = total // 2
    for role in range(2):
        acc = jnp.zeros((served, total), jnp.float32)
        for q in range(w // chunk):
            columns = pl.ds(q * chunk, chunk)
            left = noise_buf[role, :, :, columns].astype(jnp.float32).reshape(served, chunk).astype(jnp.bfloat16)
            acc = acc + lax.dot_general(
                left, full[role, :, columns], (((1,), (1,)), ((), ())), preferred_element_type=jnp.float32
            )
        acc = acc.reshape(half, 2, rows, total)
        for d in range(half):
            block = pair(b - step_of(role) * d)
            if role and not d:
                part[block] = part[block] + acc[d]
            else:
                part[block] = acc[d]
    part[pair(b + nb // 2)] = jnp.zeros((2, rows, total), jnp.float32)

    part_of = part.reshape(nf, piece, total) if piece != rows else part
    a_buf[f] = part_of[f]
    exchange(lambda k: part_of.at[lax.rem(f + k, nf)], a_buf, f, in_plane, f_order, 1)
    drain(a_buf, small_recv.at[1], nf - 1)
    own[:piece, :] = jnp.sum(a_buf[...], axis=0)
    b_buf[b] = own[...]
    exchange(lambda k: own, b_buf, b, in_column, b_order, 2)
    share(offsets[EARLY:])
    drain(b_buf, small_recv.at[2], nb - 1)
    done[...] = jnp.sum(b_buf[:, :piece, :], axis=0)
    c_buf[f] = done[...]
    exchange(lambda k: done, c_buf, f, in_plane, f_order, 3)
    norms = jnp.broadcast_to(b_buf[:, piece:, :], (nb, rows, 128))
    noise_norm = jnp.sum(jnp.where(lane == sublane, norms, 0.0), axis=2, keepdims=True).reshape(total, 1)
    data_norm = jnp.sum(jnp.where(lane == sublane + rows, norms, 0.0), axis=2, keepdims=True).reshape(total, 1)
    data_norm = jnp.transpose(jnp.broadcast_to(data_norm, (total, 128)))[:1, :]
    drain(c_buf, small_recv.at[3], nf - 1)
    cross = c_buf[...].reshape(total, total)

    scores = (2.0 * cross - noise_norm - data_norm) / root + 2.0 * root
    column = jnp.zeros((1, total), jnp.float32)
    for _ in range(ITERS):
        row = -log_count - lse(scores + column, 1)
        column = -log_count - lse(scores + row, 0)
    plan = jnp.exp(scores + row + column)
    weights = plan / jnp.sum(plan, axis=1, keepdims=True)
    wbuf[...] = weights.reshape(nb, rows, total)

    parts = 2
    step = math.gcd(512, shared // parts)
    kept = []

    def targets(chips, role, values, buf, first, count):
        blocks = []
        for d in chips:
            blocks += [wrap(sibling - step_of(role) * d), wrap(b - step_of(role) * d)]
        chosen = jnp.concatenate([wbuf[t] for t in blocks], axis=0).astype(jnp.bfloat16)
        for q in range(first, first + count, step):
            summed = jnp.dot(chosen, values[role, :, q:q + step], preferred_element_type=jnp.float32)
            buf[role, :len(blocks), :, q:q + step] = summed.reshape(len(blocks), rows, step).astype(jnp.bfloat16)

    def to_own(buf, role, place, slice_at, first, count, sem):
        where = columns_of(slice_at, first, count)
        remote(
            buf.at[role, place, :, pl.ds(first, count)], out.at[:, where],
            out_send.at[sem], out_recv.at[sem], at(sibling),
        )
        c = pltpu.make_async_copy(
            buf.at[role, place + 1, :, pl.ds(first, count)], out.at[:, where], local_sem.at[sem]
        )
        c.start()
        kept.append(c)

    def to_chips(chips, buf, slice_of, first, count, sem, roles):
        for q in range(nb // 2):
            for role in roles:
                d = lax.rem((b // 2 - q if role == 0 else q - b // 2) + nb, nb // 2)

                @pl.when((d >= max(chips[-1], 1)) & (d <= chips[0]))
                def _(q=q, role=role, d=d):
                    where = columns_of(slice_of(role, b), first, count)
                    for i, t in enumerate((2 * q + 1 - core, 2 * q + core)):
                        place = 2 * (chips[0] - d) + i
                        remote(
                            buf.at[role, place, :, pl.ds(first, count)], out.at[:, where],
                            out_send.at[sem + role], out_recv.at[sem + role], at(t),
                        )

    far = list(range(half - 1, -1, -1))
    groups = []
    if shared < w:
        for role in range(2):
            targets(far, role, full, obuf, shared, w - shared)
        to_chips(far, obuf, slice_for, shared, w - shared, 0, (0, 1))
        for role in range(2):
            to_own(obuf, role, nb // 2 - 2, slice_for(role, b), shared, w - shared, role)
            groups.append((role, shared, w - shared, nb // 2 - 1))
    for role in range(2):
        targets([0], role, full, obuf, 0, shared)
        to_own(obuf, role, 0, slice_for(role, b), 0, shared, 2 + role)
        groups.append((2 + role, 0, shared, 1))
    for role in range(2):
        drain(outer_buf.at[role], outer_recv.at[role, 0], 1)
        view = outer_buf.at[role, pl.ds(0, 2 * len(offsets)), :, pl.ds(0, shared)]
        pltpu.make_async_copy(view, view, outer_recv.at[role, 1]).wait()
    n = shared // parts
    for g in range(parts):
        for role in range(2):
            for q in range(g * n, (g + 1) * n, step):
                columns = pl.ds(q, step)
                outer_full[role, :, columns] = (
                    outer_buf[role, :, :, columns].astype(jnp.float32).reshape(total, step).astype(jnp.bfloat16)
                )
            targets(far[1:], role, outer_full, outer_obuf, g * n, n)
        sem = 4 + 2 * g
        to_chips(far[1:], outer_obuf, outer_slice, g * n, n, sem, (0, 1))
        for role in range(2):
            to_own(outer_obuf, role, nb // 2 - 4, outer_slice(role, b), g * n, n, sem + role)
            groups.append((sem + role, g * n, n, nb // 2 - 3))

    col_out[...] = column
    pot[...] = jnp.broadcast_to(row, (total, 128)).reshape(nb, rows, 128)
    row_out[...] = jnp.sum(jnp.where(lane == sublane, pot[b], 0.0), axis=0, keepdims=True)[:, :rows]

    for role in range(2):
        for d in range(half):
            drain(data_buf.at[role], first_send.at[role, d], 2 if d else 1)
            drain(data_buf.at[role], on_send.at[role, d], 2)
        for d in range(half - 1, 1, -1):
            drain(data_buf.at[role], outer_send.at[role, d], 2)
        drain(outer_buf.at[role], outer_send.at[role, 0], 1)
        view = outer_buf.at[role, pl.ds(0, 2 * len(offsets)), :, pl.ds(0, shared)]
        pltpu.make_async_copy(view, view, outer_send.at[role, 1]).wait()
        drain(noise_buf.at[role], noise_send.at[role], nb // 2 - 1)
    drain(norm_b, small_send.at[0], nf - 1)
    drain(a_buf, small_send.at[1], nf - 1)
    drain(b_buf, small_send.at[2], nb - 1)
    drain(c_buf, small_send.at[3], nf - 1)
    for sem, first, count, blocks in groups:
        view = obuf.at[0, pl.ds(0, blocks), :, pl.ds(first, count)]
        pltpu.make_async_copy(view, view, out_send.at[sem]).wait()
        pltpu.make_async_copy(view, view, out_recv.at[sem]).wait()
    for c in kept:
        c.wait()


def solution(mesh):
    nb, nf = mesh.shape["batch"], mesh.shape["feat"]

    def per_device(noise, data):
        rows, width = noise.shape
        total, w = rows * nb, width // nb
        piece = total // nf
        targets, row, column = pl.pallas_call(
            functools.partial(kernel, nb, nf),
            out_shape=(
                jax.ShapeDtypeStruct((rows, width), jnp.bfloat16),
                jax.ShapeDtypeStruct((1, rows), jnp.float32),
                jax.ShapeDtypeStruct((1, total), jnp.float32),
            ),
            in_specs=[pl.BlockSpec(memory_space=pl.ANY)] * 2,
            out_specs=[pl.BlockSpec(memory_space=pltpu.VMEM)] * 3,
            scratch_shapes=[
                pltpu.VMEM((2, nb // 2, rows, w), jnp.bfloat16),
                pltpu.VMEM((2, nb, rows, w), jnp.bfloat16),
                pltpu.VMEM((2, nb, rows, w), jnp.bfloat16),
                pltpu.VMEM((2, total, w), jnp.bfloat16),
                pltpu.VMEM((2, total, w), jnp.bfloat16),
                pltpu.VMEM((2, rows, width), jnp.bfloat16),
                pltpu.VMEM((2, nb // 2, rows, w), jnp.bfloat16),
                pltpu.VMEM((2, nb // 2 - 2, rows, w), jnp.bfloat16),
                pltpu.VMEM((nb, rows, total), jnp.float32),
                pltpu.VMEM((nf, piece, total), jnp.float32),
                pltpu.VMEM((piece + 1, total), jnp.float32),
                pltpu.VMEM((nb, piece + 1, total), jnp.float32),
                pltpu.VMEM((piece, total), jnp.float32),
                pltpu.VMEM((nf, piece, total), jnp.float32),
                pltpu.VMEM((rows, 128), jnp.float32),
                pltpu.VMEM((nf, rows, 128), jnp.float32),
                pltpu.VMEM((nb, rows, 128), jnp.float32),
                pltpu.VMEM((nb, rows, total), jnp.float32),
                pltpu.SemaphoreType.DMA((8,)),
                pltpu.SemaphoreType.DMA((2, nb // 4)),
                pltpu.SemaphoreType.DMA((2, nb // 4)),
                pltpu.SemaphoreType.DMA((2, nb // 4)),
                pltpu.SemaphoreType.DMA((2, nb // 4)),
                pltpu.SemaphoreType.DMA((2,)),
                pltpu.SemaphoreType.DMA((2,)),
                pltpu.SemaphoreType.DMA((2, nb // 4)),
                pltpu.SemaphoreType.DMA((2, nb // 4)),
                pltpu.SemaphoreType.DMA((4,)),
                pltpu.SemaphoreType.DMA((4,)),
                pltpu.SemaphoreType.DMA((8,)),
                pltpu.SemaphoreType.DMA((8,)),
            ],
            compiler_params=pltpu.CompilerParams(
                collective_id=0, has_side_effects=True, vmem_limit_bytes=52 * 2**20
            ),
        )(noise, data)
        return targets, row.reshape(rows), column.reshape(total)

    return jax.shard_map(
        per_device,
        mesh=mesh,
        in_specs=(P("batch", "feat"), P("batch", "feat")),
        out_specs=(P("batch", "feat"), P("batch"), P()),
        check_vma=False,
    )
```

time: 89.4 us -> 87.8 us (0.982); the launches traced: 88.1 us -> 87.7 us
  no operation moved by 1% of the time
where the time goes in v4:
time: 87.8 us; the launch traced here: 87.7 us
  Pallas kernels  85.1 us (97%)
  local copies, waits for them, and re-layouts  1.99 us (2%)
    pallas_call x1, Pallas kernels, per_device(): pl.pallas_call(functools.partial(kernel, nb, nf), out_shape=(jax.ShapeDty...  85.1 us
    unnamed x3, local copies, waits for them, and re-layouts  1.99 us

profile of v4, /device:TPU:1, one launch (start us, length us, event | category | flops | bytes accessed | tf_op | source)
XLA Modules:
  0.0 87.7 jit_solution(6718128111997353682)
XLA Ops:
  0.6 85.1 %shard_map.49 = (bf16[8,65536]{1,0:T(8,128)(2,1)S(1)}, f32[1,8]{1,0:T(1,128)S(1)}, f32[1,128]{1,0:T(1,128)S(1)}) custom-call(bf16[8,65536]{1,0:T(8,128)(2,1)} %noise.1, bf16[8,65536]{1,0:T(8,128)(2,1)} %data.1), custom_call_target="tpu_custom_call" | custom-call | tf_op jit(solution)/shard_map/pallas_call | solution.py:369
  85.7 1.0 %copy.8 = bf16[8,65536]{1,0:T(8,128)(2,1)} copy(bf16[8,65536]{1,0:T(8,128)(2,1)S(1)} %get-tuple-element.12) | data formatting | bytes 2097152
  86.7 0.5 copy.9
  87.2 0.5 copy.10

commit v5 on v4

--- a/solution.py
+++ b/solution.py
@@ -28,7 +28,7 @@
     noise_buf, data_buf, outer_buf, full, outer_full, local_buf, obuf, outer_obuf,
     part, a_buf, own, b_buf, done, c_buf, norm_own, norm_b, pot, wbuf,
     local_sem, outer_send, outer_recv, first_send, first_recv, noise_send, noise_recv, on_send, on_recv,
-    small_send, small_recv, out_send, out_recv,
+    small_send, small_recv, out_send, out_recv, arrived,
 ):
     rows, width = noise.shape
     w = width // nb
@@ -80,12 +80,29 @@
             src_ref=source, dst_ref=target, send_sem=send, recv_sem=recv, **device
         ).start()
 
+    side = math.isqrt(nf)
+    fy, fx = f // side, lax.rem(f, side)
+
+    def in_grid(y, x):
+        place = lax.rem(fy + y + side, side) * side + lax.rem(fx + x + side, side)
+        return dict(device_id=(b, place), device_id_type=MESH)
+
+    beside = [in_column(2), in_column(nb - 2)]
+    diagonal = [at(wrap(sibling + 2)), at(wrap(sibling - 2))]
+    row_beside = [in_grid(0, 1), in_grid(0, -1)]
+    column_beside = [in_grid(1, 0), in_grid(-1, 0)]
     barrier = pltpu.get_barrier_semaphore()
-    for k in b_order:
-        pl.semaphore_signal(barrier, inc=1, **in_column(k))
-    for k in f_order:
-        pl.semaphore_signal(barrier, inc=1, **in_plane(k))
-    pl.semaphore_wait(barrier, nb + nf - 2)
+    near = beside + diagonal + [at(sibling)] + row_beside + column_beside
+    for device in near:
+        pl.semaphore_signal(barrier, inc=1, **device)
+    pl.semaphore_wait(barrier, len(near))
+
+    def tell(devices, which):
+        for device in devices:
+            pl.semaphore_signal(arrived.at[which], inc=1, **device)
+
+    tell(beside, 0)
+    tell(row_beside, 3)
 
     for role in range(2):
         for member in (b, sibling):
@@ -93,7 +110,7 @@
                 data.at[:, columns_of(slice_for(role, member))], data_buf.at[1 - role, b],
                 on_send.at[role, 0], on_recv.at[1 - role, 0], at(wrap(member + step_of(role))),
             )
-    for d in range(half - 1, -1, -1):
+    def send_data(d):
         for role in range(2):
             for member in [sibling] if d == 0 else [
                 wrap(b + step_of(role) * d), wrap(sibling + step_of(role) * d)
@@ -108,6 +125,11 @@
                     remote(
                         source, data_buf.at[role, b], first_send.at[role, d], first_recv.at[role, d], at(member)
                     )
+    send_data(2)
+    pl.semaphore_wait(arrived.at[0], 2)
+    tell(beside, 1)
+    for d in (3, 1, 0):
+        send_data(d)
     locals_ = []
     for role in range(2):
         s = columns_of(slice_for(role, b))
@@ -136,7 +158,15 @@
                         noise_send.at[role], noise_recv.at[role], at(member),
                     )
 
+    pl.semaphore_wait(arrived.at[3], 2)
+    tell(column_beside, 4)
+    pl.semaphore_wait(arrived.at[1], 2)
+    tell(beside, 2)
     send_noise([half - 1])
+    pl.semaphore_wait(arrived.at[4], 2)
+    tell(column_beside, 5)
+    pl.semaphore_wait(arrived.at[2], 2)
+    pl.semaphore_wait(arrived.at[5], 2)
     for c in locals_:
         c.wait()
 
@@ -407,6 +437,7 @@
                 pltpu.SemaphoreType.DMA((4,)),
                 pltpu.SemaphoreType.DMA((8,)),
                 pltpu.SemaphoreType.DMA((8,)),
+                pltpu.SemaphoreType.REGULAR((6,)),
             ],
             compiler_params=pltpu.CompilerParams(
                 collective_id=0, has_side_effects=True, vmem_limit_bytes=52 * 2**20

time: 87.8 us -> 86.2 us (0.982)
  Pallas kernels: 85.1 us -> 83.5 us
    pallas_call x1, Pallas kernels: 85.1 us -> 83.5 us  [per_device(): pl.pallas_call(functools.partial(kernel, nb, nf), out_shape=(jax.ShapeDty...]
where the time goes in v5:
time: 86.2 us; the launch traced here: 86.1 us
  Pallas kernels  83.5 us (97%)
  local copies, waits for them, and re-layouts  1.99 us (2%)
    pallas_call x1, Pallas kernels, per_device(): pl.pallas_call(functools.partial(kernel, nb, nf), out_shape=(jax.ShapeDty...  83.5 us
    unnamed x3, local copies, waits for them, and re-layouts  1.99 us

profile of v5, /device:TPU:1, one launch (start us, length us, event | category | flops | bytes accessed | tf_op | source)
XLA Modules:
  0.0 86.1 jit_solution(15502772063246668604)
XLA Ops:
  0.6 83.5 %shard_map.49 = (bf16[8,65536]{1,0:T(8,128)(2,1)S(1)}, f32[1,8]{1,0:T(1,128)S(1)}, f32[1,128]{1,0:T(1,128)S(1)}) custom-call(bf16[8,65536]{1,0:T(8,128)(2,1)} %noise.1, bf16[8,65536]{1,0:T(8,128)(2,1)} %data.1), custom_call_target="tpu_custom_call" | custom-call | tf_op jit(solution)/shard_map/pallas_call | solution.py:399
  84.1 1.0 %copy.8 = bf16[8,65536]{1,0:T(8,128)(2,1)} copy(bf16[8,65536]{1,0:T(8,128)(2,1)S(1)} %get-tuple-element.12) | data formatting | bytes 2097152
  85.1 0.5 copy.9
  85.6 0.5 copy.10

commit v6 on v5

--- a/solution.py
+++ b/solution.py
@@ -10,7 +10,7 @@
 
 ITERS = 3
 SHARED = 7
-EARLY = 3
+EARLY = 2
 MESH = pl.DeviceIdType.MESH
 
 
@@ -223,17 +223,20 @@
         drain(data_buf.at[role], first_recv.at[role, 0], 1)
         for d in range(half):
             drain(data_buf.at[role], on_recv.at[role, d], 2)
-    def share(offsets):
+    def share(offsets, sem, first=0, count=shared):
+        here = pl.ds(first, count)
         for d in offsets:
             for role in range(2):
                 block = pair(b + step_of(role) * d)
                 remote(
-                    data_buf.at[role, block, :, pl.ds(0, shared)], outer_buf.at[role, block, :, pl.ds(0, shared)],
-                    outer_send.at[role, 1], outer_recv.at[role, 1], at(wrap(b - step_of(role))),
+                    data_buf.at[role, block, :, here], outer_buf.at[role, block, :, here],
+                    outer_send.at[role, sem], outer_recv.at[role, sem], at(wrap(b - step_of(role))),
                 )
 
     offsets = list(range(half + 1))
-    share(offsets[:EARLY])
+    early, late = offsets[:EARLY], offsets[EARLY:]
+    share(early, 1)
+    share(late[:1], half, 0, shared // 2)
 
     chunk = min(1024, w)
     for role in range(2):
@@ -246,15 +249,17 @@
         drain(noise_buf.at[role], noise_recv.at[role], nb // 2 - 1)
 
     served = total // 2
-    for role in range(2):
-        acc = jnp.zeros((served, total), jnp.float32)
-        for q in range(w // chunk):
-            columns = pl.ds(q * chunk, chunk)
+    accs = [jnp.zeros((served, total), jnp.float32)] * 2
+    chunk = min(1024, w)
+    for q in range(w // chunk):
+        columns = pl.ds(q * chunk, chunk)
+        for role in range(2):
             left = noise_buf[role, :, :, columns].astype(jnp.float32).reshape(served, chunk).astype(jnp.bfloat16)
-            acc = acc + lax.dot_general(
+            accs[role] = accs[role] + lax.dot_general(
                 left, full[role, :, columns], (((1,), (1,)), ((), ())), preferred_element_type=jnp.float32
             )
-        acc = acc.reshape(half, 2, rows, total)
+    for role in range(2):
+        acc = accs[role].reshape(half, 2, rows, total)
         for d in range(half):
             block = pair(b - step_of(role) * d)
             if role and not d:
@@ -270,7 +275,27 @@
     own[:piece, :] = jnp.sum(a_buf[...], axis=0)
     b_buf[b] = own[...]
     exchange(lambda k: own, b_buf, b, in_column, b_order, 2)
-    share(offsets[EARLY:])
+    share(late[:1], half, shared // 2, shared // 2)
+    share(late[1:], half)
+
+    def outer_pairs(devices, roles=(0, 1)):
+        for role in roles:
+            for device in devices(role):
+                block = pair(device)
+                at_row = pl.ds(pl.multiple_of(wrap(device) // 2 * (2 * rows), 2 * rows), 2 * rows)
+                outer_full[role, at_row, :shared] = (
+                    outer_buf[role, block, :, :shared].astype(jnp.float32)
+                    .reshape(2 * rows, shared).astype(jnp.bfloat16)
+                )
+
+    def arrival(kind, sem, count, roles=(0, 1)):
+        for role in roles:
+            view = outer_buf.at[role, pl.ds(0, 2 * count), :, pl.ds(0, shared)]
+            pltpu.make_async_copy(view, view, kind.at[role, sem]).wait()
+
+    for role in range(2):
+        drain(outer_buf.at[role], outer_recv.at[role, 0], 1)
+    outer_pairs(lambda role: [b - step_of(role) * d for d in range(half - 1)])
     drain(b_buf, small_recv.at[2], nb - 1)
     done[...] = jnp.sum(b_buf[:, :piece, :], axis=0)
     c_buf[f] = done[...]
@@ -279,6 +304,8 @@
     noise_norm = jnp.sum(jnp.where(lane == sublane, norms, 0.0), axis=2, keepdims=True).reshape(total, 1)
     data_norm = jnp.sum(jnp.where(lane == sublane + rows, norms, 0.0), axis=2, keepdims=True).reshape(total, 1)
     data_norm = jnp.transpose(jnp.broadcast_to(data_norm, (total, 128)))[:1, :]
+    arrival(outer_recv, 1, len(early))
+    outer_pairs(lambda role: [b + step_of(role) * (d + 1) for d in early])
     drain(c_buf, small_recv.at[3], nf - 1)
     cross = c_buf[...].reshape(total, total)
 
@@ -291,8 +318,7 @@
     weights = plan / jnp.sum(plan, axis=1, keepdims=True)
     wbuf[...] = weights.reshape(nb, rows, total)
 
-    parts = 2
-    step = math.gcd(512, shared // parts)
+    step = math.gcd(512, shared)
     kept = []
 
     def targets(chips, role, values, buf, first, count):
@@ -332,36 +358,26 @@
                         )
 
     far = list(range(half - 1, -1, -1))
-    groups = []
-    if shared < w:
-        for role in range(2):
-            targets(far, role, full, obuf, shared, w - shared)
-        to_chips(far, obuf, slice_for, shared, w - shared, 0, (0, 1))
-        for role in range(2):
-            to_own(obuf, role, nb // 2 - 2, slice_for(role, b), shared, w - shared, role)
-            groups.append((role, shared, w - shared, nb // 2 - 1))
-    for role in range(2):
+    for role in range(2):
+        targets(far, role, full, obuf, shared, w - shared)
+    to_chips(far, obuf, slice_for, shared, w - shared, 0, (0, 1))
+    for role in range(2):
+        arrival(outer_recv, half, len(late), (role,))
+        outer_pairs(lambda role: [b + step_of(role) * (d + 1) for d in late], (role,))
+        targets(far[1:], role, outer_full, outer_obuf, 0, shared)
+        to_chips(far[1:], outer_obuf, outer_slice, 0, shared, 4, (role,))
+    for role in range(2):
+        to_own(outer_obuf, role, nb // 2 - 4, outer_slice(role, b), 0, shared, 4 + role)
+        to_own(obuf, role, nb // 2 - 2, slice_for(role, b), shared, w - shared, role)
         targets([0], role, full, obuf, 0, shared)
         to_own(obuf, role, 0, slice_for(role, b), 0, shared, 2 + role)
-        groups.append((2 + role, 0, shared, 1))
-    for role in range(2):
-        drain(outer_buf.at[role], outer_recv.at[role, 0], 1)
-        view = outer_buf.at[role, pl.ds(0, 2 * len(offsets)), :, pl.ds(0, shared)]
-        pltpu.make_async_copy(view, view, outer_recv.at[role, 1]).wait()
-    n = shared // parts
-    for g in range(parts):
-        for role in range(2):
-            for q in range(g * n, (g + 1) * n, step):
-                columns = pl.ds(q, step)
-                outer_full[role, :, columns] = (
-                    outer_buf[role, :, :, columns].astype(jnp.float32).reshape(total, step).astype(jnp.bfloat16)
-                )
-            targets(far[1:], role, outer_full, outer_obuf, g * n, n)
-        sem = 4 + 2 * g
-        to_chips(far[1:], outer_obuf, outer_slice, g * n, n, sem, (0, 1))
-        for role in range(2):
-            to_own(outer_obuf, role, nb // 2 - 4, outer_slice(role, b), g * n, n, sem + role)
-            groups.append((sem + role, g * n, n, nb // 2 - 3))
+    groups = [
+        (role + sem, first, count, blocks)
+        for role in range(2)
+        for sem, first, count, blocks in (
+            (0, shared, w - shared, nb // 2 - 1), (2, 0, shared, 1), (4, 0, shared, nb // 2 - 3)
+        )
+    ]
 
     col_out[...] = column
     pot[...] = jnp.broadcast_to(row, (total, 128)).reshape(nb, rows, 128)
@@ -374,9 +390,9 @@
         for d in range(half - 1, 1, -1):
             drain(data_buf.at[role], outer_send.at[role, d], 2)
         drain(outer_buf.at[role], outer_send.at[role, 0], 1)
-        view = outer_buf.at[role, pl.ds(0, 2 * len(offsets)), :, pl.ds(0, shared)]
-        pltpu.make_async_copy(view, view, outer_send.at[role, 1]).wait()
         drain(noise_buf.at[role], noise_send.at[role], nb // 2 - 1)
+    arrival(outer_send, 1, len(early))
+    arrival(outer_send, half, len(late))
     drain(norm_b, small_send.at[0], nf - 1)
     drain(a_buf, small_send.at[1], nf - 1)
     drain(b_buf, small_send.at[2], nb - 1)
@@ -425,8 +441,8 @@
                 pltpu.VMEM((nb, rows, 128), jnp.float32),
                 pltpu.VMEM((nb, rows, total), jnp.float32),
                 pltpu.SemaphoreType.DMA((8,)),
-                pltpu.SemaphoreType.DMA((2, nb // 4)),
-                pltpu.SemaphoreType.DMA((2, nb // 4)),
+                pltpu.SemaphoreType.DMA((2, nb // 4 + 1)),
+                pltpu.SemaphoreType.DMA((2, nb // 4 + 1)),
                 pltpu.SemaphoreType.DMA((2, nb // 4)),
                 pltpu.SemaphoreType.DMA((2, nb // 4)),
                 pltpu.SemaphoreType.DMA((2,)),

time: 86.2 us -> 85.3 us (0.990); the launches traced: 86.1 us -> 84 us
  Pallas kernels: 83.5 us -> 81.4 us
    pallas_call x1, Pallas kernels: 83.5 us -> 81.4 us  [per_device(): pl.pallas_call(functools.partial(kernel, nb, nf), out_shape=(jax.ShapeDty...]
where the time goes in v6:
time: 85.3 us; the launch traced here: 84 us
  Pallas kernels  81.4 us (95%)
  local copies, waits for them, and re-layouts  1.99 us (2%)
    pallas_call x1, Pallas kernels, per_device(): pl.pallas_call(functools.partial(kernel, nb, nf), out_shape=(jax.ShapeDty...  81.4 us
    unnamed x3, local copies, waits for them, and re-layouts  1.99 us

profile of v6, /device:TPU:1, one launch (start us, length us, event | category | flops | bytes accessed | tf_op | source)
XLA Modules:
  0.0 84.0 jit_solution(3555242718092867773)
XLA Ops:
  0.6 81.4 %shard_map.49 = (bf16[8,65536]{1,0:T(8,128)(2,1)S(1)}, f32[1,8]{1,0:T(1,128)S(1)}, f32[1,128]{1,0:T(1,128)S(1)}) custom-call(bf16[8,65536]{1,0:T(8,128)(2,1)} %noise.1, bf16[8,65536]{1,0:T(8,128)(2,1)} %data.1), custom_call_target="tpu_custom_call" | custom-call | tf_op jit(solution)/shard_map/pallas_call | solution.py:415
  82.0 1.0 %copy.8 = bf16[8,65536]{1,0:T(8,128)(2,1)} copy(bf16[8,65536]{1,0:T(8,128)(2,1)S(1)} %get-tuple-element.12) | data formatting | bytes 2097152
  83.0 0.5 copy.9
  83.5 0.5 copy.10

commit v7 on v6

--- a/solution.py
+++ b/solution.py
@@ -17,6 +17,11 @@
 def lse(values, axis):
     top = jnp.max(values, axis=axis, keepdims=True)
     return top + jnp.log(jnp.sum(jnp.exp(values - top), axis=axis, keepdims=True))
+
+
+def plane_order(side):
+    steps = [(y, x) for y in range(side) for x in range(side) if y or x]
+    return sorted(steps, key=lambda s: -min(s[0], side - s[0]) - min(s[1], side - s[1]))
 
 
 def far_first(count):
@@ -42,7 +47,9 @@
     b, f = lax.axis_index("batch"), lax.axis_index("feat")
     core = lax.rem(b, 2)
     sibling = b + 1 - 2 * core
-    b_order, f_order = far_first(nb), list(range(1, nf))
+    side = math.isqrt(nf)
+    b_order, f_order = far_first(nb), plane_order(side)
+    fy, fx = f // side, lax.rem(f, side)
 
     def at(t):
         return dict(device_id=(t, f), device_id_type=MESH)
@@ -50,8 +57,14 @@
     def in_column(k):
         return at(lax.rem(b + k, nb))
 
+    def place_at(y, x):
+        return lax.rem(fy + y + side, side) * side + lax.rem(fx + x + side, side)
+
+    def in_grid(y, x):
+        return dict(device_id=(b, place_at(y, x)), device_id_type=MESH)
+
     def in_plane(k):
-        return dict(device_id=(b, lax.rem(f + k, nf)), device_id_type=MESH)
+        return in_grid(*k)
 
     def drain(ref, sem, count):
         view = ref.at[pl.ds(0, count)]
@@ -79,13 +92,6 @@
         pltpu.make_async_remote_copy(
             src_ref=source, dst_ref=target, send_sem=send, recv_sem=recv, **device
         ).start()
-
-    side = math.isqrt(nf)
-    fy, fx = f // side, lax.rem(f, side)
-
-    def in_grid(y, x):
-        place = lax.rem(fy + y + side, side) * side + lax.rem(fx + x + side, side)
-        return dict(device_id=(b, place), device_id_type=MESH)
 
     beside = [in_column(2), in_column(nb - 2)]
     diagonal = [at(wrap(sibling + 2)), at(wrap(sibling - 2))]
@@ -270,7 +276,7 @@
 
     part_of = part.reshape(nf, piece, total) if piece != rows else part
     a_buf[f] = part_of[f]
-    exchange(lambda k: part_of.at[lax.rem(f + k, nf)], a_buf, f, in_plane, f_order, 1)
+    exchange(lambda k: part_of.at[place_at(*k)], a_buf, f, in_plane, f_order, 1)
     drain(a_buf, small_recv.at[1], nf - 1)
     own[:piece, :] = jnp.sum(a_buf[...], axis=0)
     b_buf[b] = own[...]
@@ -344,7 +350,7 @@
 
     def to_chips(chips, buf, slice_of, first, count, sem, roles):
         for q in range(nb // 2):
-            for role in roles:
+            for role in roles[::-1]:
                 d = lax.rem((b // 2 - q if role == 0 else q - b // 2) + nb, nb // 2)
 
                 @pl.when((d >= max(chips[-1], 1)) & (d <= chips[0]))
@@ -403,6 +409,12 @@
         pltpu.make_async_copy(view, view, out_recv.at[sem]).wait()
     for c in kept:
         c.wait()
+
+
+def place(targets, row, column, targets_out, row_out, column_out, sem):
+    targets_out[...] = targets[...]
+    row_out[...] = row[...]
+    column_out[...] = column[...]
 
 
 def solution(mesh):
@@ -459,6 +471,19 @@
                 collective_id=0, has_side_effects=True, vmem_limit_bytes=52 * 2**20
             ),
         )(noise, data)
+        inside = pl.BlockSpec(memory_space=pltpu.VMEM)
+        targets, row, column = pl.pallas_call(
+            place,
+            out_shape=(
+                jax.ShapeDtypeStruct((rows, width), jnp.bfloat16),
+                jax.ShapeDtypeStruct((1, rows), jnp.float32),
+                jax.ShapeDtypeStruct((1, total), jnp.float32),
+            ),
+            in_specs=[inside] * 3,
+            out_specs=(inside, inside, inside),
+            scratch_shapes=[pltpu.SemaphoreType.DMA],
+            compiler_params=pltpu.CompilerParams(vmem_limit_bytes=52 * 2**20),
+        )(targets, row, column)
         return targets, row.reshape(rows), column.reshape(total)
 
     return jax.shard_map(

time: 85.3 us -> 84.2 us (0.987)
  local copies, waits for them, and re-layouts: 1.99 us -> 0 us
    unnamed x3 -> x0, local copies, waits for them, and re-layouts: 1.99 us -> none
    pallas_call x0 -> x1, Pallas kernels: none -> 1.05 us  [per_device(): pl.pallas_call(place, out_shape=(jax.ShapeDtypeStruct((rows, width), jnp....]
where the time goes in v7:
time: 84.2 us; the launch traced here: 82.6 us
  Pallas kernels  82 us (97%)
    pallas_call x1, Pallas kernels, per_device(): pl.pallas_call(functools.partial(kernel, nb, nf), out_shape=(jax.ShapeDty...  80.9 us

profile of v7, /device:TPU:1, one launch (start us, length us, event | category | flops | bytes accessed | tf_op | source)
XLA Modules:
  0.0 82.6 jit_solution(16669534565937118514)
XLA Ops:
  0.6 80.9 %shard_map.49 = (bf16[8,65536]{1,0:T(8,128)(2,1)S(1)}, f32[1,8]{1,0:T(1,128)S(1)}, f32[1,128]{1,0:T(1,128)S(1)}) custom-call(bf16[8,65536]{1,0:T(8,128)(2,1)} %noise.1, bf16[8,65536]{1,0:T(8,128)(2,1)} %data.1), custom_call_target="tpu_custom_call" | custom-call | tf_op jit(solution)/shard_map/pallas_call | solution.py:427
  81.5 1.1 %shard_map.50 = (bf16[8,65536]{1,0:T(8,128)(2,1)}, f32[1,8]{1,0:T(1,128)}, f32[1,128]{1,0:T(1,128)}) custom-call(bf16[8,65536]{1,0:T(8,128)(2,1)S(1)} %get-tuple-element.9.targets, f32[1,8]{1,0:T(1,128)S(1)} %get-tuple-element.10.row, f32[1,128]{1,0:T(1,128)S(1)} %get-tuple-element.11.column), custom_call_target="tpu_custom_call" | custom-call | tf_op jit(solution)/shard_map/pallas_call | solution.py:475

commit v8 on v7

--- a/solution.py
+++ b/solution.py
@@ -412,7 +412,9 @@
 
 
 def place(targets, row, column, targets_out, row_out, column_out, sem):
-    targets_out[...] = targets[...]
+    n = targets_out.shape[1]
+    here = pl.ds(pl.multiple_of(pl.program_id(0) * n, n), n)
+    targets_out[...] = targets[:, here]
     row_out[...] = row[...]
     column_out[...] = column[...]
 
@@ -480,7 +482,8 @@
                 jax.ShapeDtypeStruct((1, total), jnp.float32),
             ),
             in_specs=[inside] * 3,
-            out_specs=(inside, inside, inside),
+            grid=(2,),
+            out_specs=(pl.BlockSpec((rows, width // 2), lambda i: (0, i)), inside, inside),
             scratch_shapes=[pltpu.SemaphoreType.DMA],
             compiler_params=pltpu.CompilerParams(vmem_limit_bytes=52 * 2**20),
         )(targets, row, column)

time: 84.2 us -> 84.1 us (level)
  no operation moved by 1% of the time
where the time goes in v8:
time: 84.1 us; the launch traced here: 82.6 us
  Pallas kernels  81.9 us (97%)
    pallas_call x1, Pallas kernels, per_device(): pl.pallas_call(functools.partial(kernel, nb, nf), out_shape=(jax.ShapeDty...  80.9 us

profile of v8, /device:TPU:1, one launch (start us, length us, event | category | flops | bytes accessed | tf_op | source)
XLA Modules:
  0.0 82.6 jit_solution(10316366010213263541)
XLA Ops:
  0.6 80.9 %shard_map.49 = (bf16[8,65536]{1,0:T(8,128)(2,1)S(1)}, f32[1,8]{1,0:T(1,128)S(1)}, f32[1,128]{1,0:T(1,128)S(1)}) custom-call(bf16[8,65536]{1,0:T(8,128)(2,1)} %noise.1, bf16[8,65536]{1,0:T(8,128)(2,1)} %data.1), custom_call_target="tpu_custom_call" | custom-call | tf_op jit(solution)/shard_map/pallas_call | solution.py:429
  81.5 1.0 %shard_map.50 = (bf16[8,65536]{1,0:T(8,128)(2,1)}, f32[1,8]{1,0:T(1,128)}, f32[1,128]{1,0:T(1,128)}) custom-call(bf16[8,65536]{1,0:T(8,128)(2,1)S(1)} %get-tuple-element.9.targets, f32[1,8]{1,0:T(1,128)S(1)} %get-tuple-element.10.row, f32[1,128]{1,0:T(1,128)S(1)} %get-tuple-element.11.column), custom_call_target="tpu_custom_call" | custom-call | tf_op jit(solution)/shard_map/pallas_call | solution.py:477
